TPU v7x, 128 devices: a whole 4x4x4 slice. The times are simulated.
128 devices in a mesh: dp: 8 (over z_hi, y), tensor: 16 (over x, z_lo, core).
Axes of the slice: x: 4, y: 4, z: 4 (z_hi: 2, z_lo: 2; z = z_hi * 2 + z_lo), core: 2. Of those that a mesh axis runs over, the one named last changes fastest.
Arguments:
- hidden: bfloat16 [4096, 53248], P('dp', 'tensor'), may hold values from -6 to 6
- cotangent: bfloat16 [4096, 16384], P('dp', 'tensor'), may hold values from -96 to 96
- prompt_group_index: int32 [4096], P('dp'), may hold values from 0 to 511
- answer_token_mask: int32 [4096], P('dp'), may hold values 0 or 1
- token_reward_order: int32 [4096], P('dp'), may hold values from 0 to 15
- source_lowdim_matrix: float32 [32, 53248], P(None, 'tensor'), may hold values from -0.02734375 to 0.02734375
- running_mean_source_matrix: float32 [32, 53248], P(None, 'tensor'), may hold values from -6 to 6
- running_variance_source_matrix: float32 [32, 53248], P(None, 'tensor'), may hold values from 0.01 to 1
- target_lowdim_matrix: float32 [32, 16384], P(None, 'tensor'), may hold values from -1 to 1
- running_mean_target_matrix: float32 [32, 16384], P(None, 'tensor'), may hold values from -0.6 to 0.6
- running_variance_target_matrix: float32 [32, 16384], P(None, 'tensor'), may hold values from 0.0001 to 0.01
- frozen_down_weight: bfloat16 [53248, 16384], P('tensor', 'dp'), may hold values from -0.02734375 to 0.02734375
- sampled_token_input: bfloat16 [512, 53248], P(None, 'tensor'), may hold values from -6 to 6
Outputs:
- rollout_out: bfloat16 [512, 16384], P(None, ('dp', 'tensor'))
- next_left_factor: float32 [32, 53248], P('dp', 'tensor')
- next_first_moment_left: float32 [32, 53248], P('dp', 'tensor')
- next_second_moment_left: float32 [32, 53248], P('dp', 'tensor')
- next_right_factor: float32 [32, 16384], P('dp', 'tensor')
- next_first_moment_right: float32 [32, 16384], P('dp', 'tensor')
- next_second_moment_right: float32 [32, 16384], P('dp', 'tensor')
All inputs are finite; a program needn't handle non-finite values. No bound on the sum of `answer_token_mask` on one device may be relied on, other than what follows from the above.
Results may differ from a plain program's by a relative error of at most 0.0063.
Values may be sent and summed in bfloat16 or wider, within the bound.
A program may use at most 128 MiB of HBM per device.

v0:
```python
import jax
import jax.numpy as jnp
from jax import lax
from jax.sharding import PartitionSpec as P

adapter_scale = 2.0
bias_one = 1.0 - 0.9**10
bias_two = 1.0 - 0.999**10


def adaptive_moment_step(param, grad, first, second):
    first = 0.9 * first + 0.1 * grad
    second = 0.999 * second + 0.001 * grad * grad
    param = param - 0.004 * (first / bias_one) / (jnp.sqrt(second / bias_two) + 1e-08)
    return (param, first, second)


def own_rows(array, count):
    return lax.dynamic_slice_in_dim(array, lax.axis_index("dp") * count, count, 0)


def shards(
    hidden,
    cotangent,
    prompt_group_index,
    answer_token_mask,
    token_reward_order,
    source_lowdim_matrix,
    running_mean_source_matrix,
    running_variance_source_matrix,
    target_lowdim_matrix,
    running_mean_target_matrix,
    running_variance_target_matrix,
    frozen_down_weight,
    sampled_token_input,
):
    replica_count = lax.axis_size("dp")
    left_factor_value = source_lowdim_matrix.astype(jnp.bfloat16)
    partial_proj = lax.dot_general(
        hidden, left_factor_value, (((1,), (1,)), ((), ())), preferred_element_type=jnp.float32
    )
    rank_projection = lax.psum(partial_proj, "tensor")
    group_count = hidden.shape[0] * replica_count // 8
    mask_float = answer_token_mask.astype(jnp.float32)
    rank_float = token_reward_order.astype(jnp.float32)
    member = (
        prompt_group_index[:, None] == jnp.arange(group_count, dtype=jnp.int32)[None, :]
    ).astype(jnp.float32)
    masked = member * mask_float[:, None]
    counts = jnp.sum(masked, axis=0)
    sums = jnp.sum(masked * rank_float[:, None], axis=0)
    squares = jnp.sum(masked * (rank_float * rank_float)[:, None], axis=0)
    counts, sums, squares = lax.psum((counts, sums, squares), "dp")
    safe_counts = jnp.maximum(counts, 1.0)
    mean = sums / safe_counts
    spread = jnp.maximum(jnp.sqrt(jnp.maximum(squares / safe_counts - mean * mean, 0.0)), 1.0)
    total = jnp.maximum(jnp.sum(counts), 1.0)
    table = jnp.stack([mean, spread], axis=1)
    looked = jnp.dot(member, table, precision=lax.Precision.HIGHEST)
    coefficient = -mask_float * (rank_float - looked[:, 0]) / looked[:, 1] / total
    incoming_gradient = coefficient[:, None] * cotangent.astype(jnp.float32)
    local_backward_gradient = jnp.dot(
        incoming_gradient, target_lowdim_matrix.T, precision=lax.Precision.HIGHEST
    )
    backward_gradient = lax.psum(local_backward_gradient, "tensor").astype(jnp.bfloat16)
    left_factor_gradient = adapter_scale * lax.dot_general(
        backward_gradient, hidden, (((0,), (0,)), ((), ())), preferred_element_type=jnp.float32
    )
    right_factor_gradient = adapter_scale * lax.dot_general(
        rank_projection,
        incoming_gradient,
        (((0,), (0,)), ((), ())),
        precision=lax.Precision.HIGHEST,
    )
    local_rank_slice = source_lowdim_matrix.shape[0] // replica_count
    left_factor_gradient, right_factor_gradient = lax.psum(
        (left_factor_gradient, right_factor_gradient), "dp"
    )
    next_left_factor, next_first_moment_left, next_second_moment_left = adaptive_moment_step(
        source_lowdim_matrix,
        left_factor_gradient,
        running_mean_source_matrix,
        running_variance_source_matrix,
    )
    next_right_factor, next_first_moment_right, next_second_moment_right = adaptive_moment_step(
        target_lowdim_matrix,
        right_factor_gradient,
        running_mean_target_matrix,
        running_variance_target_matrix,
    )
    a_send = next_left_factor.astype(jnp.bfloat16)
    b_send = next_right_factor.astype(jnp.bfloat16)
    next_left_factor = own_rows(next_left_factor, local_rank_slice)
    next_first_moment_left = own_rows(next_first_moment_left, local_rank_slice)
    next_second_moment_left = own_rows(next_second_moment_left, local_rank_slice)
    next_right_factor = own_rows(next_right_factor, local_rank_slice)
    next_first_moment_right = own_rows(next_first_moment_right, local_rank_slice)
    next_second_moment_right = own_rows(next_second_moment_right, local_rank_slice)
    b_whole = lax.all_gather(b_send, "tensor", axis=1, tiled=True)
    block_cols = frozen_down_weight.shape[1]
    b_block = lax.dynamic_slice_in_dim(b_whole, lax.axis_index("dp") * block_cols, block_cols, 1)
    adapter_product = lax.dot_general(
        a_send, b_block, (((0,), (0,)), ((), ())), preferred_element_type=jnp.float32
    )
    combined_weight = (
        frozen_down_weight.astype(jnp.float32) + adapter_scale * adapter_product
    ).astype(jnp.bfloat16)
    partial_out = jnp.dot(sampled_token_input, combined_weight, preferred_element_type=jnp.float32)
    rollout_out = lax.psum_scatter(partial_out, "tensor", scatter_dimension=1, tiled=True).astype(
        jnp.bfloat16
    )
    return (
        rollout_out,
        next_left_factor,
        next_first_moment_left,
        next_second_moment_left,
        next_right_factor,
        next_first_moment_right,
        next_second_moment_right,
    )


def solution(mesh):
    placed = (
        P("dp", "tensor"),
        P("dp", "tensor"),
        P("dp"),
        P("dp"),
        P("dp"),
        P(None, "tensor"),
        P(None, "tensor"),
        P(None, "tensor"),
        P(None, "tensor"),
        P(None, "tensor"),
        P(None, "tensor"),
        P("tensor", "dp"),
        P(None, "tensor"),
    )
    return jax.shard_map(
        shards,
        mesh=mesh,
        in_specs=placed,
        out_specs=(
            P(None, ("dp", "tensor")),
            P("dp", "tensor"),
            P("dp", "tensor"),
            P("dp", "tensor"),
            P("dp", "tensor"),
            P("dp", "tensor"),
            P("dp", "tensor"),
        ),
        check_vma=False,
    )
```

profile of v0, /device:TPU:1, one launch (start us, length us, event | category | flops | bytes accessed | tf_op | source)
XLA Modules:
  0.0 328.9 jit_solution(10265599472039974748)
XLA Ops:
  7.3 3.9 %fusion.12 = f32[512,32]{0,1:T(8,128)} fusion(bf16[512,3328]{1,0:T(8,128)(2,1)} %param.13, f32[32,3328]{1,0:T(8,128)} %param.18), kind=kOutput, calls=%fused_computation.22 | convolution fusion | flops 109158400 | bytes 3899392 | tf_op jit(solution)/shard_map/dot_general | solution.py:39
  11.3 1.0 fusion.5
  12.3 23.2 %all-reduce = (f32[512]{0:T(512)}, f32[512]{0:T(512)}, f32[512]{0:T(512)}) all-reduce(f32[512]{0:T(512)S(1)} %get-tuple-element.30, f32[512]{0:T(512)S(1)} %get-tuple-element.29, f32[512]{0:T(512)S(1)} %get-tuple-element.28), channel_id=1, replica_groups=mesh['dp'=8,'tensor'=16] {'dp'}, use_global_device_ids=true, to_apply=%region_5.0 | all-reduce | flops 1536 | bytes 12288 | tf_op jit(solution)/shard_map/psum | solution.py:53
  35.5 1.3 maximum_divide_fusion
  37.5 1.3 fusion.9
  38.8 0.7 multiply_divide_fusion
  39.5 4.1 %fusion.3 = f32[512,32]{0,1:T(8,128)} fusion(f32[32,1024]{1,0:T(8,128)S(1)} %copy-done.1, bf16[512,1024]{1,0:T(8,128)(2,1)} %param.14, f32[512]{0:T(512)S(1)} %multiply_divide_fusion), kind=kOutput, calls=%fused_computation.6 | convolution fusion | flops 202375168 | bytes 1247232 | tf_op jit(solution)/shard_map/dot_general | solution.py:62
  43.6 54.1 %psum.52 = bf16[512,32]{0,1:T(8,128)(2,1)} all-reduce(f32[512,32]{0,1:T(8,128)} %fusion.3), channel_id=1, replica_groups=mesh['dp'=8,'tensor'=16] {'tensor'}, use_global_device_ids=true, to_apply=%region_7.0 | all-reduce | flops 16384 | bytes 98304 | tf_op jit(solution)/shard_map/psum | solution.py:65
  97.6 3.4 %convolution_multiply_fusion = f32[32,3328]{1,0:T(8,128)} fusion(bf16[512,3328]{1,0:T(8,128)(2,1)} %param.13, bf16[512,32]{0,1:T(8,128)(2,1)} %psum.52), kind=kOutput, calls=%fused_computation.2 | convolution fusion | flops 109158400 | bytes 3866624 | tf_op jit(solution)/shard_map/dot_general | solution.py:66
  101.1 17.8 %all-reduce.5.cloned.1.call-done = f32[512,32]{0,1:T(8,128)} async-done(((f32[512,32]{0,1:T(8,128)}), f32[512,32]{0,1:T(8,128)}) %all-reduce.5.cloned.1.call-update) | async-done | bytes 65552 | tf_op jit(solution)/shard_map/psum | solution.py:42
  118.8 3.4 %fusion.4 = f32[32,1024]{1,0:T(8,128)} fusion(f32[512,32]{0,1:T(8,128)} %all-reduce.5.cloned.1.call-done, bf16[512,1024]{1,0:T(8,128)(2,1)} %param.14, f32[512]{0:T(512)S(1)} %multiply_divide_fusion), kind=kOutput, calls=%fused_computation.10 | convolution fusion | flops 202407936 | bytes 1247232 | tf_op jit(solution)/shard_map/dot_general | solution.py:69
  122.3 0.0 all-gather.2.cloned.1.call-start
  122.3 80.9 %all-reduce.7.cloned.1.call-done = (f32[32,3328]{1,0:T(8,128)}, f32[32,1024]{1,0:T(8,128)}) async-done(((f32[32,3328]{1,0:T(8,128)}, f32[32,1024]{1,0:T(8,128)}), (f32[32,3328]{1,0:T(8,128)}, f32[32,1024]{1,0:T(8,128)})) %all-reduce.7.cloned.1.call-update) | async-done | bytes 557072 | tf_op jit(solution)/shard_map/psum | solution.py:76
  203.2 1.8 fusion.27
  205.1 2.6 divide_subtract_fusion
  207.7 33.7 %all-gather.2.cloned.1.call-done = bf16[32,16384]{1,0:T(8,128)(2,1)} async-done(((bf16[32,1024]{1,0:T(8,128)(2,1)}), bf16[32,16384]{1,0:T(8,128)(2,1)}) %all-gather.2.cloned.1.call-update) | async-done | bytes 1048592 | tf_op jit(solution)/shard_map/all_gather | solution.py:99
  241.4 15.3 %fusion.1 = f32[512,2048]{0,1:T(8,128)} fusion(bf16[512,3328]{1,0:T(8,128)(2,1)S(1)} %copy-done, bf16[3328,2048]{1,0:T(8,128)(2,1)} %param.24, f32[32,3328]{1,0:T(8,128)} %get-tuple-element.40, bf16[32,16384]{1,0:T(8,128)(2,1)} %all-gather.2.cloned.1.call-done, s32[]{:T(128)S(6)} %select_n.4), kind=kOutput, calls=%fused_computation.3 | convolution fusion | flops 7442898944 | bytes 21790724 | tf_op jit(solution)/shard_map/dot_general | solution.py:108
  256.8 1.4 constant_dynamic-slice_fusion.2
  258.1 1.4 constant_dynamic-slice_fusion
  259.5 1.5 constant_dynamic-slice_fusion.5
  261.1 1.6 constant_dynamic-slice_fusion.3
  262.7 58.0 %reduce-scatter.2.cloned.1.call-done = f32[512,128]{0,1:T(8,128)} async-done(((f32[512,2048]{0,1:T(8,128)}), f32[512,128]{0,1:T(8,128)}) %reduce-scatter.2.cloned.1.call-update) | async-done | bytes 262160 | tf_op jit(solution)/shard_map/reduce_scatter | solution.py:109
  320.7 1.0 convert_element_type.40
  321.6 0.8 copy.22
  (19 shorter events, 0.2 us)
Async XLA Ops:
  7.2 234.3 %copy-start = (bf16[512,3328]{1,0:T(8,128)(2,1)S(1)}, bf16[512,3328]{1,0:T(8,128)(2,1)}, u32[]{:S(2)}) copy-start(bf16[512,3328]{1,0:T(8,128)(2,1)} %param.25) | copy-start | bytes 10223620
  7.2 4.0 %copy-start.2 = (s32[512]{0:T(512)S(1)}, s32[512]{0:T(512)}, u32[]{:S(2)}) copy-start(s32[512]{0:T(512)} %param.17) | copy-start | bytes 6148
  7.2 4.1 %copy-start.3 = (s32[512]{0:T(512)S(1)}, s32[512]{0:T(512)}, u32[]{:S(2)}) copy-start(s32[512]{0:T(512)} %param.16) | copy-start | bytes 6148
  7.2 32.3 %copy-start.1 = (f32[32,1024]{1,0:T(8,128)S(1)}, f32[32,1024]{1,0:T(8,128)}, u32[]{:S(2)}) copy-start(f32[32,1024]{1,0:T(8,128)} %param.21) | copy-start | bytes 393220
  7.2 111.6 %all-reduce.5.cloned.1.call-start = ((), (), s32[]{:S(2)}) async-start(), calls=%async_computation.1 | async-start | bytes 131072 | tf_op jit(solution)/shard_map/psum | solution.py:42
  11.2 192.0 %all-reduce.7.cloned.1.call-start = ((), (), s32[]{:S(2)}) async-start(), calls=%async_computation.4 | async-start | bytes 1114112 | tf_op jit(solution)/shard_map/psum | solution.py:76
  122.3 119.2 %all-gather.2.cloned.1.call-start = ((), (), s32[]{:S(2)}) async-start(), calls=%async_computation.2 | async-start | bytes 1114112 | tf_op jit(solution)/shard_map/all_gather | solution.py:99
  205.0 115.6 %reduce-scatter.2.cloned.1.call-start = ((), (), s32[]{:S(2)}) async-start(), calls=%async_computation.3 | async-start | bytes 4456448 | tf_op jit(solution)/shard_map/reduce_scatter | solution.py:109
Sparse Core Ops, SparseCore 0:
  11.3 107.4 all-reduce.4
  122.4 80.7 all-reduce.6
  205.2 36.2 all-gather.1
  256.9 63.7 reduce-scatter.1
where the time goes:
time: 332 us; the launch traced here: 329 us
  waiting for transfers between devices  190 us (57%)
  blocking collectives  77.2 us (23%)
  matrix products  31.4 us (9%)
  between operations  14.5 us (4%)
  other arithmetic  8.48 us (3%)
  local copies, waits for them, and re-layouts  6.68 us (2%)
    psum x1, waiting for transfers between devices, shards(): lax.psum((left_factor_gradient, right_factor_gradient), 'dp')  80.9 us
    reduce_scatter x1, waiting for transfers between devices, shards(): lax.psum_scatter(partial_out, 'tensor', scatter_dimension=1, tiled=True)  58 us
    psum x1, blocking collectives, shards(): lax.psum(local_backward_gradient, 'tensor').astype(jnp.bfloat16)  54.1 us
    all_gather x1, waiting for transfers between devices, shards(): b_whole = lax.all_gather(b_send, 'tensor', axis=1, tiled=True)  33.7 us
    psum x1, blocking collectives, shards(): counts, sums, squares = lax.psum((counts, sums, squares), 'dp')  23.2 us
    psum x1, waiting for transfers between devices, shards(): rank_projection = lax.psum(partial_proj, 'tensor')  17.8 us
    dot_general x1, matrix products, shards(): jnp.dot(sampled_token_input, combined_weight, preferred_element_type=jnp....  15.3 us
  transfers between devices with their start and end apart: 4, of which 4 were waited for; matrix products, arithmetic and copies ran while one was open for 6% of the time, Pallas kernels for 0%

commit v1 on v0

v1 whole, which is shorter than its diff:
```python
import functools

import jax
import jax.numpy as jnp
from jax import lax
from jax.experimental import pallas as pl
from jax.experimental.pallas import tpu as pltpu
from jax.sharding import PartitionSpec as P

MESH = pl.DeviceIdType.MESH
F32 = jnp.float32
BF16 = jnp.bfloat16

adapter_scale = 2.0
bias_one = 1.0 - 0.9**10
bias_two = 1.0 - 0.999**10

GAP_ONE, GAP_TWO = 2, 4


def contract(left, right, left_dim, right_dim):
    return lax.dot_general(
        left, right, (((left_dim,), (right_dim,)), ((), ())), preferred_element_type=F32
    )


def high_low(value):
    high = value.astype(BF16)
    return high, (value - high.astype(F32)).astype(BF16)


def quarters(value, width):
    return jnp.concatenate([value[:, q * width : (q + 1) * width] for q in range(4)], axis=0)


def kernel(
    nd, nt,
    hidden, cotangent, groups, mask, order, a_in, ma_in, va_in, b_in, mb_in, vb_in, weight, sampled,
    out, pa_out, ma_out, va_out, pb_out, mb_out, vb_out,
    hid, cot, grp, msk, odr, a, ma, va, b, mb, vb, w, x,
    stat, stat_r, coef, s1, r1, full, g, gf, gs, gr, own, xa_s, xa_r, xall, bs, bd,
    keep, give, got, big, big_r,
    o_out, o_pa, o_ma, o_va, o_pb, o_mb, o_vb,
    lsem, wsem, osem, pair_sem, got_sem, big_sem, big_rsem, bs_sem, chain_sem,
):
    i = lax.axis_index("dp")
    t = lax.axis_index("tensor")
    core = lax.rem(t, 2)
    chip = t // 2
    chips = nt // 2
    half_rows = chip * 8
    inner = hid.shape[1]
    width = cot.shape[1]
    quarter = gs.shape[2]
    n_tok = hid.shape[0]
    half_tok = n_tok // 2

    b_home = t // 8
    own_b = jnp.logical_and(t // 2 == i, t - 8 * core >= 0)
    own_b = jnp.logical_and(own_b, t - 8 * core < 8)
    b_source = 2 * i + b_home
    barrier = pltpu.get_barrier_semaphore()

    def greet_tensor(d, _):
        pl.semaphore_signal(
            barrier, inc=1, device_id={"tensor": lax.rem(t + d, nt)}, device_id_type=MESH
        )
        return _

    def greet_dp(d, _):
        pl.semaphore_signal(
            barrier, inc=1, device_id={"dp": lax.rem(i + d, nd)}, device_id_type=MESH
        )
        return _

    def greet_source(r, carry):
        @pl.when(jnp.logical_or(r != i, b_source != t))
        def _():
            pl.semaphore_signal(
                barrier, inc=1, device_id={"dp": r, "tensor": b_source}, device_id_type=MESH
            )

        return carry

    loads = [
        (groups, grp), (mask, msk), (order, odr), (a_in, a), (b_in, b), (cotangent, cot),
    ]
    load = [pltpu.make_async_copy(src, dst, lsem.at[n]) for n, (src, dst) in enumerate(loads)]
    for copy in load:
        copy.start()
    pieces = 2
    piece = inner // pieces
    hid_load = []
    for n in range(pieces):
        cols = pl.ds(n * piece, piece)
        hid_load.append(
            pltpu.make_async_copy(hidden.at[:, cols], hid.at[:, cols], lsem.at[6 + n])
        )
        hid_load[-1].start()

    lax.fori_loop(1, nt, greet_tensor, 0)
    lax.fori_loop(1, nd, greet_dp, 0)
    lax.fori_loop(0, nd, greet_source, 0)

    x_load = pltpu.make_async_copy(sampled, x, lsem.at[8])

    def block_of(s):
        return lax.rem(chip + 1 + s, chips)

    def w_load(s):
        cols = pl.ds(pl.multiple_of(block_of(s) * 256, 256), 256)
        return pltpu.make_async_copy(weight.at[:, cols], w.at[s], wsem.at[s])

    late = [
        pltpu.make_async_copy(src, dst, lsem.at[9 + n])
        for n, (src, dst) in enumerate([(ma_in, ma), (va_in, va), (mb_in, mb), (vb_in, vb)])
    ]

    for n in range(3):
        load[n].wait()
    mask_row = msk[...].astype(F32)
    rank_row = odr[...].astype(F32)
    n_groups = stat.shape[1]
    group_id = lax.broadcasted_iota(jnp.int32, (n_groups, n_tok), 0)
    member = jnp.where(group_id == grp[...], 1.0, 0.0).astype(BF16)
    row = lax.broadcasted_iota(jnp.int32, (8, n_tok), 0)
    weighted = mask_row * rank_row
    terms = jnp.where(
        row == 0, mask_row, jnp.where(row == 1, weighted, jnp.where(row == 2, weighted * rank_row, 0.0))
    )
    stat[...] = contract(terms.astype(BF16), member, 1, 1)

    load[4].wait()
    load[5].wait()
    b_high, b_low = high_low(b[...])
    raw = contract(jnp.concatenate([b_high, b_low], axis=0), cot[...], 1, 1)
    s1[32:64, :] = raw[0:32] + raw[32:64]

    pl.semaphore_wait(barrier, (nt - 1) + (nd - 1) + 8 - own_b.astype(jnp.int32))

    def to_dp(src, dst, sems):
        def body(d, _):
            pltpu.make_async_remote_copy(
                src_ref=src(lax.rem(i + d, nd)), dst_ref=dst(d),
                send_sem=chain_sem.at[sems], recv_sem=chain_sem.at[sems + 1],
                device_id={"dp": lax.rem(i + d, nd)}, device_id_type=MESH,
            ).start()
            return _

        lax.fori_loop(1, nd, body, 0)

    def to_tensor(src, dst, sems):
        def body(d, _):
            pltpu.make_async_remote_copy(
                src_ref=src(lax.rem(t + d, nt)), dst_ref=dst(d),
                send_sem=chain_sem.at[sems], recv_sem=chain_sem.at[sems + 1],
                device_id={"tensor": lax.rem(t + d, nt)}, device_id_type=MESH,
            ).start()
            return _

        lax.fori_loop(1, nt, body, 0)

    def arrived(ref, sems):
        pltpu.make_async_copy(ref, ref, chain_sem.at[sems + 1]).wait()

    def sent(ref, sems):
        pltpu.make_async_copy(ref, ref, chain_sem.at[sems]).wait()

    to_dp(lambda r: stat, lambda d: stat_r.at[d - 1], 0)

    load[3].wait()
    a_half = a[...].astype(BF16)
    total = None
    for n in range(pieces):
        hid_load[n].wait()
        if n == 0:
            x_load.start()
            for s in range(2):
                w_load(s).start()
        cols = slice(n * piece, (n + 1) * piece)
        part = contract(a_half[:, cols], hid[:, cols], 1, 1)
        total = part if total is None else total + part
    for s in range(2, chips):
        w_load(s).start()
    for copy in late:
        copy.start()
    s1[0:32, :] = total

    def chunk(ref, k):
        rows = pl.ds(pl.multiple_of((k // 2) * 8, 8), 8)
        cols = pl.ds(pl.multiple_of(lax.rem(k, 2) * half_tok, half_tok), half_tok)
        return ref.at[rows, cols]

    to_tensor(lambda k: chunk(s1, k), lambda d: r1.at[d - 1], 2)

    def partner(t):
        return t + 1 - 2 * core

    def pair_copy(s):
        return pltpu.make_async_remote_copy(
            src_ref=give.at[s], dst_ref=got.at[s], send_sem=pair_sem.at[s], recv_sem=got_sem.at[s],
            device_id={"tensor": partner(t)}, device_id_type=MESH,
        )

    def compute(s, _):
        w_load(s).wait()
        block = contract(x[...], w[s], 1, 0)
        first, second = block[:, :128], block[:, 128:]
        keep[s] = jnp.where(core == 0, first, second)
        give[s] = jnp.where(core == 0, second, first).astype(BF16)
        pair_copy(s).start()
        return _

    def big_copy(s):
        return pltpu.make_async_remote_copy(
            src_ref=big.at[s], dst_ref=big_r.at[s], send_sem=big_sem.at[s], recv_sem=big_rsem.at[s],
            device_id={"tensor": 2 * block_of(s) + core}, device_id_type=MESH,
        )

    def forward(s, _):
        pair_copy(s).wait_recv()
        big[s] = (keep[s] + got[s].astype(F32)).astype(BF16)
        big_copy(s).start()
        return _

    x_load.wait()
    lax.fori_loop(0, GAP_ONE, compute, 0)

    arrived(stat_r, 0)
    stats = stat[...]
    for d in range(nd - 1):
        stats = stats + stat_r[d]
    counts, sums, squares = stats[0:1], stats[1:2], stats[2:3]
    safe = jnp.maximum(counts, 1.0)
    mean = sums / safe
    spread = jnp.maximum(jnp.sqrt(jnp.maximum(squares / safe - mean * mean, 0.0)), 1.0)
    every = jnp.maximum(jnp.sum(counts, axis=1, keepdims=True), 1.0)
    table = jnp.zeros((8, n_groups), F32)
    row_g = lax.broadcasted_iota(jnp.int32, (8, n_groups), 0)
    for base, value in ((0, mean), (3, spread)):
        rest = value
        for n in range(3):
            term = rest.astype(BF16).astype(F32)
            table = jnp.where(row_g == base + n, term, table)
            rest = rest - term
    looked = contract(table.astype(BF16), member, 1, 0)
    mean_t = (looked[0:1] + looked[1:2]) + looked[2:3]
    spread_t = (looked[3:4] + looked[4:5]) + looked[5:6]
    coef[...] = jnp.broadcast_to(-mask_row * (rank_row - mean_t) / spread_t / every, (8, n_tok))

    arrived(r1, 2)
    mine = chunk(s1, t)[...]
    for d in range(nt - 1):
        mine = mine + r1[d]
    half = pl.ds(pl.multiple_of(core * half_tok, half_tok), half_tok)
    full_mine = chunk(full, t)
    full_mine[...] = mine * coef[:, half]
    to_tensor(lambda k: chunk(full, t), lambda d: chunk(full, t), 4)

    lax.fori_loop(GAP_ONE, GAP_TWO, compute, 0)

    for copy in late:
        copy.wait()

    def own_rows(value_a, value_b, slot):
        rows = pl.ds(pl.multiple_of((i // 2) * 8, 8), 8)
        odd = lax.rem(i, 2) == 1

        def pick(ref):
            eight = ref[rows, :]
            return jnp.where(odd, eight[4:8], eight[0:4])

        pad = jnp.zeros((4, 4 * quarter - inner - width), F32)
        own[slot] = quarters(jnp.concatenate([pick(value_a), pick(value_b), pad], axis=1), quarter)

    own_rows(a, b, 0)
    own_rows(ma, mb, 1)
    own_rows(va, vb, 2)

    arrived(r1, 4)
    back = full[32:64, :].astype(BF16)
    p_high, p_low = high_low(full[0:32, :])
    g[:, 0:inner] = adapter_scale * contract(back, hid[...], 1, 0)
    right = contract(jnp.concatenate([p_high, p_low], axis=0), cot[...], 1, 0)
    g[:, inner : inner + width] = adapter_scale * (right[0:32] + right[32:64])
    g[:, inner + width :] = jnp.zeros((32, 4 * quarter - inner - width), F32)
    for r in range(nd):
        value = quarters(g[4 * r : 4 * r + 4, :], quarter)
        gf[r] = value
        gs[r] = value.astype(BF16)
    to_dp(lambda r: gs.at[r], lambda d: gr.at[d - 1], 6)

    lax.fori_loop(0, GAP_ONE, forward, 0)

    def both(s, _):
        compute(s, 0)
        forward(s - (GAP_TWO - GAP_ONE), 0)
        return _

    lax.fori_loop(GAP_TWO, chips, both, 0)

    arrived(gr, 6)
    grad = gf[i]
    for d in range(nd - 1):
        grad = grad + gr[d].astype(F32)
    first = 0.9 * own[1] + 0.1 * grad
    second = 0.999 * own[2] + 0.001 * grad * grad
    param = own[0] - 0.004 * (first / bias_one) / (jnp.sqrt(second / bias_two) + 1e-08)
    a_send = param.astype(BF16)
    rounded = a_send.astype(F32)
    for k in range(8):
        at = inner + 128 * k
        q, c = at // quarter, at % quarter
        part = rounded[4 * q : 4 * q + 4, c : c + 128]
        bs[k] = jnp.concatenate([part, part], axis=0)

    def b_copy(k):
        return pltpu.make_async_remote_copy(
            src_ref=bs.at[k], dst_ref=bd.at[i], send_sem=bs_sem.at[k], recv_sem=chain_sem.at[12],
            device_id={"dp": t // 2, "tensor": 8 * core + k}, device_id_type=MESH,
        )

    def b_here(k):
        return jnp.logical_and(t // 2 == i, 8 * core + k == t)

    def send_b(k, carry):
        @pl.when(jnp.logical_not(b_here(k)))
        def _():
            b_copy(k).start()

        @pl.when(b_here(k))
        def _():
            pltpu.make_async_copy(bs.at[k], bd.at[i], chain_sem.at[12]).start()

        return carry

    partial = None
    for q in range(4):
        cols = min(quarter, inner - q * quarter)
        if cols <= 0:
            continue
        part = contract(a_send[:, :cols], x[:, q * quarter : q * quarter + cols], 1, 1)
        part = part[4 * q : 4 * q + 4]
        partial = part if partial is None else partial + part
    xa_s[...] = jnp.concatenate([partial[:, :half_tok], partial[:, half_tok:]], axis=0)
    to_tensor(lambda k: xa_s, lambda d: xa_r.at[d - 1], 8)
    lax.fori_loop(0, 8, send_b, 0)

    def split(value, left_ref, right_ref):
        for q in range(4):
            lo, hi = q * quarter, (q + 1) * quarter
            rows = value[4 * q : 4 * q + 4]
            if lo < inner:
                left_ref[:, lo : min(hi, inner)] = rows[:, : min(hi, inner) - lo]
            start, stop = max(lo, inner), min(hi, inner + width)
            if start < stop:
                right_ref[:, start - inner : stop - inner] = rows[:, start - lo : stop - lo]

    split(param, o_pa, o_pb)
    split(first, o_ma, o_mb)
    split(second, o_va, o_vb)
    outs = [
        (o_pa, pa_out), (o_ma, ma_out), (o_va, va_out), (o_pb, pb_out), (o_mb, mb_out), (o_vb, vb_out),
    ]
    stores = [pltpu.make_async_copy(src, dst, osem.at[n]) for n, (src, dst) in enumerate(outs)]
    for copy in stores:
        copy.start()

    lax.fori_loop(chips - (GAP_TWO - GAP_ONE), chips - 1, forward, 0)

    arrived(xa_r, 8)
    mine = xa_s[...]
    for d in range(nt - 1):
        mine = mine + xa_r[d]
    xall[i] = mine
    to_dp(lambda r: xall.at[i], lambda d: xall.at[i], 10)

    pair_copy(chips - 1).wait_recv()
    keep[chips - 1] = keep[chips - 1] + got[chips - 1].astype(F32)
    for s in range(chips - 1):
        big_copy(s).wait_recv()
    summed = keep[chips - 1]
    for s in range(chips - 1):
        summed = summed + big_r[s].astype(F32)
    keep[chips - 1] = summed

    pltpu.make_async_copy(bd, bd, chain_sem.at[12]).wait()
    pltpu.make_async_copy(xa_r.at[pl.ds(0, nd - 1)], xa_r.at[pl.ds(0, nd - 1)], chain_sem.at[11]).wait()
    z_high, z_low = high_low(xall[...].reshape(8 * nd, half_tok))
    z = jnp.concatenate([z_high, z_low], axis=0)
    b_rows = bd[...].reshape(8 * nd, 128)
    row_b = lax.rem(lax.broadcasted_iota(jnp.int32, (8 * nd, 128), 0), 8)
    for h in range(2):
        b_half = jnp.where((row_b < 4) == (h == 0), b_rows, 0.0).astype(BF16)
        added = contract(z, jnp.concatenate([b_half, b_half], axis=0), 0, 0)
        rows = slice(h * half_tok, (h + 1) * half_tok)
        o_out[rows, :] = (keep[chips - 1, rows, :] + adapter_scale * added).astype(BF16)
    last = pltpu.make_async_copy(o_out, out, osem.at[6])
    last.start()

    sent(stat_r, 0)
    sent(r1, 2)
    sent(r1, 4)
    sent(gr, 6)
    sent(xa_r, 8)
    sent(xa_r.at[pl.ds(0, nd - 1)], 10)
    for s in range(chips):
        pair_copy(s).wait_send()
    for s in range(chips - 1):
        big_copy(s).wait_send()

    def b_sent(k, carry):
        @pl.when(jnp.logical_not(b_here(k)))
        def _():
            b_copy(k).wait_send()

        return carry

    lax.fori_loop(0, 8, b_sent, 0)
    for copy in stores:
        copy.wait()
    last.wait()


def shards(
    hidden, cotangent, prompt_group_index, answer_token_mask, token_reward_order,
    source_lowdim_matrix, running_mean_source_matrix, running_variance_source_matrix,
    target_lowdim_matrix, running_mean_target_matrix, running_variance_target_matrix,
    frozen_down_weight, sampled_token_input,
):
    nd, nt = lax.axis_size("dp"), lax.axis_size("tensor")
    tokens, inner = hidden.shape
    width = cotangent.shape[1]
    rank = source_lowdim_matrix.shape[0]
    columns = frozen_down_weight.shape[1]
    rollout = sampled_token_input.shape[0]
    n_groups = tokens * nd // 8
    chips = nt // 2
    quarter = -(-(inner + width) // 512) * 128
    rows = rank // nd
    vmem, dma = pltpu.VMEM, pltpu.SemaphoreType.DMA
    i32 = jnp.int32
    scratch = [
        vmem((tokens, inner), BF16), vmem((tokens, width), BF16),
        vmem((1, tokens), i32), vmem((1, tokens), i32), vmem((1, tokens), i32),
        vmem((rank, inner), F32), vmem((rank, inner), F32), vmem((rank, inner), F32),
        vmem((rank, width), F32), vmem((rank, width), F32), vmem((rank, width), F32),
        vmem((chips, inner, 256), BF16), vmem((rollout, inner), BF16),
        vmem((8, n_groups), F32), vmem((nd - 1, 8, n_groups), F32), vmem((8, tokens), F32),
        vmem((64, tokens), F32), vmem((nt - 1, 8, tokens // 2), F32), vmem((64, tokens), F32),
        vmem((rank, 4 * quarter), F32), vmem((nd, 16, quarter), F32), vmem((nd, 16, quarter), BF16),
        vmem((nd - 1, 16, quarter), BF16), vmem((3, 16, quarter), F32),
        vmem((8, rollout // 2), F32), vmem((nt - 1, 8, rollout // 2), F32),
        vmem((nd, 8, rollout // 2), F32), vmem((8, 8, 128), F32), vmem((nd, 8, 128), F32),
        vmem((chips, rollout, 128), F32), vmem((chips, rollout, 128), BF16),
        vmem((chips, rollout, 128), BF16), vmem((chips - 1, rollout, 128), BF16),
        vmem((chips - 1, rollout, 128), BF16),
        vmem((rollout, 128), BF16),
        vmem((rows, inner), F32), vmem((rows, inner), F32), vmem((rows, inner), F32),
        vmem((rows, width), F32), vmem((rows, width), F32), vmem((rows, width), F32),
        dma((13,)), dma((chips,)), dma((7,)), dma((chips,)), dma((chips,)),
        dma((chips - 1,)), dma((chips - 1,)), dma((8,)), dma((13,)),
    ]
    left = jax.ShapeDtypeStruct((rows, inner), F32)
    right = jax.ShapeDtypeStruct((rows, width), F32)
    return pl.pallas_call(
        functools.partial(kernel, nd, nt),
        out_shape=(jax.ShapeDtypeStruct((rollout, 128), BF16), left, left, left, right, right, right),
        in_specs=[pl.BlockSpec(memory_space=pl.ANY)] * 13,
        out_specs=[pl.BlockSpec(memory_space=pl.ANY)] * 7,
        scratch_shapes=scratch,
        compiler_params=pltpu.CompilerParams(
            collective_id=0, has_side_effects=True, vmem_limit_bytes=60 * 2**20
        ),
        name="grpo_step",
    )(
        hidden, cotangent,
        prompt_group_index.reshape(1, tokens), answer_token_mask.reshape(1, tokens),
        token_reward_order.reshape(1, tokens),
        source_lowdim_matrix, running_mean_source_matrix, running_variance_source_matrix,
        target_lowdim_matrix, running_mean_target_matrix, running_variance_target_matrix,
        frozen_down_weight, sampled_token_input,
    )


def solution(mesh):
    factor = P(None, "tensor")
    placed = (
        P("dp", "tensor"), P("dp", "tensor"), P("dp"), P("dp"), P("dp"),
        factor, factor, factor, factor, factor, factor, P("tensor", "dp"), factor,
    )
    owned = P("dp", "tensor")
    return jax.shard_map(
        shards,
        mesh=mesh,
        in_specs=placed,
        out_specs=(P(None, ("dp", "tensor")), owned, owned, owned, owned, owned, owned),
        check_vma=False,
    )
```

time: 332 us -> 56.2 us (0.17)
  waiting for transfers between devices: 190 us -> 0 us
  blocking collectives: 77.2 us -> 0 us
  Pallas kernels: 0 us -> 45 us
  matrix products: 31.4 us -> 0 us
  between operations: 14.5 us -> 0.65 us
  other arithmetic: 8.48 us -> 0 us
    psum x2 -> x0, waiting for transfers between devices: 98.6 us -> none  [the longest x1 80.9 us: shards(): lax.psum((left_factor_gradient, right_factor_gradient), 'dp')]
    psum x2 -> x0, blocking collectives: 77.2 us -> none  [the longest x1 54.1 us: shards(): lax.psum(local_backward_gradient, 'tensor').astype(jnp.bfloat16)]
    reduce_scatter x1 -> x0, waiting for transfers between devices: 58 us -> none  [shards(): lax.psum_scatter(partial_out, 'tensor', scatter_dimension=1, tiled=True)]
    pallas_call x0 -> x1, Pallas kernels: none -> 45 us  [shards(): pl.pallas_call(functools.partial(kernel, nd, nt), out_shape=(jax.ShapeDty...]
    all_gather x1 -> x0, waiting for transfers between devices: 33.7 us -> none  [shards(): b_whole = lax.all_gather(b_send, 'tensor', axis=1, tiled=True)]
    dot_general x6 -> x0, matrix products: 31.4 us -> none  [the longest x1 15.3 us: shards(): jnp.dot(sampled_token_input, combined_weight, preferred_element_type=jnp....]
    unnamed x9 -> x7, local copies, waits for them, and re-layouts: 0.78 us -> 9.84 us
    dynamic_slice x4 -> x0, local copies, waits for them, and re-layouts: 5.9 us -> none  [own_rows(): lax.dynamic_slice_in_dim(array, lax.axis_index('dp') * count, count, 0)]
  transfers between devices with their start and end apart: 4 -> 0, of which waited for: 4 -> 0; matrix products, arithmetic and copies ran while one was open for 6% -> 0% of each run, Pallas kernels for 0% -> 0%
where the time goes in v1:
time: 56.2 us; the launch traced here: 55.5 us
  Pallas kernels  45 us (80%)
  local copies, waits for them, and re-layouts  9.84 us (18%)
  between operations  0.65 us (1%)
    pallas_call x1, Pallas kernels, shards(): pl.pallas_call(functools.partial(kernel, nd, nt), out_shape=(jax.ShapeDty...  45 us
    unnamed x7, local copies, waits for them, and re-layouts  9.84 us

profile of v1, /device:TPU:1, one launch (start us, length us, event | category | flops | bytes accessed | tf_op | source)
XLA Modules:
  0.0 55.5 jit_solution(7489001873946777493)
XLA Ops:
  0.6 45.0 %grpo_step.1 = (bf16[512,128]{1,0:T(8,128)(2,1)}, f32[4,3328]{1,0:T(4,128)}, f32[4,3328]{1,0:T(4,128)}, f32[4,3328]{1,0:T(4,128)}, f32[4,1024]{1,0:T(4,128)}, /*index=5*/f32[4,1024]{1,0:T(4,128)}, f32[4,1024]{1,0:T(4,128)}) custom-call(bf16[512,3328]{1,0:T(8,128)(2,1)} %hidden.1, bf16[512,1024]{1,0:T(8,128)(2,1)} %cotangent.1, s32[1,512]{1,0:T(1,128)} %bitcast.3, ...), custom_call_target="tpu_custom_call" | custom-call | tf_op jit(solution)/shard_map/grpo_step/pallas_call | solution.py:466
  45.6 1.6 %copy.27 = bf16[512,128]{1,0:T(8,128)(2,1)} copy(bf16[512,128]{1,0:T(8,128)(2,1)} %get-tuple-element.14) | data formatting | bytes 262144
  47.2 1.4 %copy.28 = f32[4,3328]{1,0:T(4,128)} copy(f32[4,3328]{1,0:T(4,128)} %get-tuple-element.15) | data formatting | bytes 106496
  48.6 1.4 %copy.29 = f32[4,3328]{1,0:T(4,128)} copy(f32[4,3328]{1,0:T(4,128)} %get-tuple-element.16) | data formatting | bytes 106496
  50.1 1.4 %copy.30 = f32[4,3328]{1,0:T(4,128)} copy(f32[4,3328]{1,0:T(4,128)} %get-tuple-element.17) | data formatting | bytes 106496
  51.5 1.3 %copy.31 = f32[4,1024]{1,0:T(4,128)} copy(f32[4,1024]{1,0:T(4,128)} %get-tuple-element.18) | data formatting | bytes 32768
  52.8 1.3 %copy.32 = f32[4,1024]{1,0:T(4,128)} copy(f32[4,1024]{1,0:T(4,128)} %get-tuple-element.19) | data formatting | bytes 32768
  54.1 1.3 %copy.33 = f32[4,1024]{1,0:T(4,128)} copy(f32[4,1024]{1,0:T(4,128)} %get-tuple-element.20) | data formatting | bytes 32768

commit v2 on v1

v2 whole, which is shorter than its diff:
```python
import functools

import jax
import jax.numpy as jnp
from jax import lax
from jax.experimental import pallas as pl
from jax.experimental.pallas import tpu as pltpu
from jax.sharding import PartitionSpec as P

MESH = pl.DeviceIdType.MESH
F32 = jnp.float32
BF16 = jnp.bfloat16

adapter_scale = 2.0
bias_one = 1.0 - 0.9**10
bias_two = 1.0 - 0.999**10

BLOCKS = ((2, 0), (2, 1), (1, 0), (3, 1), (1, 1), (3, 0), (0, 1), (0, 0))
GAP_ONE, GAP_TWO = 3, 4
FAR = ((2, 1), (1, 1), (3, 1), (2, 0), (0, 1), (1, 0), (3, 0))


def contract(left, right, left_dim, right_dim):
    return lax.dot_general(
        left, right, (((left_dim,), (right_dim,)), ((), ())), preferred_element_type=F32
    )


def high_low(value):
    high = value.astype(BF16)
    return high, (value - high.astype(F32)).astype(BF16)


def quarters(value, width):
    return jnp.concatenate([value[:, q * width : (q + 1) * width] for q in range(4)], axis=0)


def kernel(
    nd, nt,
    hidden, cotangent, groups, mask, order, a_in, ma_in, va_in, b_in, mb_in, vb_in, weight, sampled,
    o_out, o_pa, o_ma, o_va, o_pb, o_mb, o_vb,
    hid, cot, grp, msk, odr, a, ma, va, b, mb, vb, w, x,
    stat, stat_r, s1, cr, cs, ar, full, g, gf, gs, gr, own, xa_s, xa_r, xall, bs, bc, bd,
    keep, give, got, part_s, part_r,
    lsem, wsem, pair_sem, got_sem, part_sem, part_rsem, b_sem, chain_sem,
):
    i = lax.axis_index("dp")
    t = lax.axis_index("tensor")
    core = lax.rem(t, 2)
    place = t // 4
    level = lax.rem(t // 2, 2)
    chips = nt // 2
    inner = hid.shape[1]
    width = cot.shape[1]
    quarter = gs.shape[2]
    n_tok = hid.shape[0]
    half_tok = n_tok // 2

    def tensor_peer(dx, dz, dc):
        return lax.rem(place + dx, 4) * 4 + lax.rem(level + dz, 2) * 2 + lax.rem(core + dc, 2)

    def dp_peer(dy, dz):
        return lax.rem(i // 4 + dz, 2) * 4 + lax.rem(lax.rem(i, 4) + dy, 4)

    same_core = [(dx, dz, 0) for dx, dz in FAR]
    tensor_all = [(dx, dz, dc) for dx, dz in FAR for dc in (1, 0)] + [(0, 0, 1)]

    def load(src, dst, n):
        copy = pltpu.make_async_copy(src, dst, lsem.at[n])
        copy.start()
        return copy

    small = [load(groups, grp, 0), load(mask, msk, 1), load(order, odr, 2)]
    b_load = load(b_in, b, 3)
    a_load = load(a_in, a, 4)
    cot_load = load(cotangent, cot, 5)
    pieces = 2
    piece = inner // pieces
    hid_load = []
    for n in range(pieces):
        cols = pl.ds(n * piece, piece)
        hid_load.append(load(hidden.at[:, cols], hid.at[:, cols], 6 + n))

    barrier = pltpu.get_barrier_semaphore()
    for dx, dz, dc in tensor_all:
        pl.semaphore_signal(
            barrier, inc=1, device_id={"tensor": tensor_peer(dx, dz, dc)}, device_id_type=MESH
        )
    for dy, dz in FAR:
        pl.semaphore_signal(barrier, inc=1, device_id={"dp": dp_peer(dy, dz)}, device_id_type=MESH)

    def w_load(s):
        dx, dz = BLOCKS[s]
        block = lax.rem(place + dx, 4) * 2 + lax.rem(level + dz, 2)
        cols = pl.ds(pl.multiple_of(block * 256, 256), 256)
        pltpu.make_async_copy(weight.at[:, cols], w.at[s], wsem.at[s]).start()

    for copy in small:
        copy.wait()
    mask_row = msk[...].astype(F32)
    rank_row = odr[...].astype(F32)
    n_groups = stat.shape[1]
    group_id = lax.broadcasted_iota(jnp.int32, (n_groups, n_tok), 0)
    member = jnp.where(group_id == grp[...], 1.0, 0.0).astype(BF16)
    row = lax.broadcasted_iota(jnp.int32, (8, n_tok), 0)
    weighted = mask_row * rank_row
    terms = jnp.where(
        row == 0, mask_row, jnp.where(row == 1, weighted, jnp.where(row == 2, weighted * rank_row, 0.0))
    )
    stat[...] = contract(terms.astype(BF16), member, 1, 1)

    b_load.wait()
    cot_load.wait()
    b_high, b_low = high_low(b[...])
    raw = contract(jnp.concatenate([b_high, b_low], axis=0), cot[...], 1, 1)
    s1[32:64, :] = raw[0:32] + raw[32:64]

    a_load.wait()
    a_half = a[...].astype(BF16)
    total = None
    for n in range(pieces):
        hid_load[n].wait()
        if n == 0:
            x_load = load(sampled, x, 8)
            for s in range(2):
                w_load(s)
        cols = slice(n * piece, (n + 1) * piece)
        part = contract(a_half[:, cols], hid[:, cols], 1, 1)
        total = part if total is None else total + part
    s1[0:32, :] = total
    for s in range(2, chips):
        w_load(s)
    late = [load(ma_in, ma, 9), load(va_in, va, 10), load(mb_in, mb, 11), load(vb_in, vb, 12)]

    pl.semaphore_wait(barrier, len(tensor_all) + len(FAR))

    def copy_to(src, dst, send, recv, peer):
        return pltpu.make_async_remote_copy(
            src_ref=src, dst_ref=dst, send_sem=send, recv_sem=recv, device_id=peer, device_id_type=MESH
        )

    def to_dp(src, dst, sems):
        for n, (dy, dz) in enumerate(FAR):
            peer = dp_peer(dy, dz)
            copy_to(
                src(peer), dst(n), chain_sem.at[sems], chain_sem.at[sems + 1], {"dp": peer}
            ).start()

    def to_tensor(src, dst, sems, peers):
        for n, (dx, dz, dc) in enumerate(peers):
            copy_to(
                src, dst(n), chain_sem.at[sems], chain_sem.at[sems + 1],
                {"tensor": tensor_peer(dx, dz, dc)},
            ).start()

    def arrived(ref, sems):
        pltpu.make_async_copy(ref, ref, chain_sem.at[sems + 1]).wait()

    def sent(ref, sems):
        pltpu.make_async_copy(ref, ref, chain_sem.at[sems]).wait()

    other = {"tensor": tensor_peer(0, 0, 1)}
    theirs = pl.ds(pl.multiple_of(32 - 32 * core, 32), 32)
    ours = pl.ds(pl.multiple_of(32 * core, 32), 32)
    chip_copy = copy_to(s1.at[theirs], cr, chain_sem.at[2], chain_sem.at[3], other)
    chip_copy.start()
    to_dp(lambda peer: stat, lambda n: stat_r.at[n], 0)
    chip_copy.wait_recv()
    chip_sum = s1[ours, :] + cr[...]
    s1[ours, :] = chip_sum
    cs[...] = chip_sum.astype(BF16)
    to_tensor(cs, lambda n: ar.at[n], 4, same_core)

    def pair_copy(s):
        return copy_to(give.at[s], got.at[s], pair_sem.at[s], got_sem.at[s], other)

    def compute(s, carry):
        pltpu.make_async_copy(weight.at[:, pl.ds(0, 256)], w.at[s], wsem.at[s]).wait()
        block = contract(x[...], w[s], 1, 0)
        first, second = block[:, :128], block[:, 128:]
        keep[s] = jnp.where(core == 0, first, second)
        give[s] = jnp.where(core == 0, second, first).astype(BF16)
        pair_copy(s).start()
        return carry

    def chip_total(s):
        pair_copy(s).wait_recv()
        return keep[s] + got[s].astype(F32)

    ahead = {"tensor": tensor_peer(1, 0, 0)}
    behind = {"tensor": tensor_peer(3, 0, 0)}
    across = {"tensor": tensor_peer(0, 1, 0)}
    routes = (ahead, behind, ahead, behind, ahead, behind, across)

    def part_copy(n):
        return copy_to(part_s.at[n], part_r.at[n], part_sem.at[n], part_rsem.at[n], routes[n])

    def forward(n, value):
        part_s[n] = value.astype(BF16)
        part_copy(n).start()

    def received(n):
        part_copy(n).wait_recv()
        return part_r[n].astype(F32)

    x_load.wait()
    lax.fori_loop(0, GAP_ONE, compute, 0)

    arrived(stat_r, 0)
    stats = stat[...]
    for d in range(nd - 1):
        stats = stats + stat_r[d]
    counts, sums, squares = stats[0:1], stats[1:2], stats[2:3]
    safe = jnp.maximum(counts, 1.0)
    mean = sums / safe
    spread = jnp.maximum(jnp.sqrt(jnp.maximum(squares / safe - mean * mean, 0.0)), 1.0)
    every = jnp.maximum(jnp.sum(counts, axis=1, keepdims=True), 1.0)
    table = jnp.zeros((8, n_groups), F32)
    row_g = lax.broadcasted_iota(jnp.int32, (8, n_groups), 0)
    for base, value in ((0, mean), (3, spread)):
        rest = value
        for n in range(3):
            term = rest.astype(BF16).astype(F32)
            table = jnp.where(row_g == base + n, term, table)
            rest = rest - term
    looked = contract(table.astype(BF16), member, 1, 0)
    mean_t = (looked[0:1] + looked[1:2]) + looked[2:3]
    spread_t = (looked[3:4] + looked[4:5]) + looked[5:6]
    coefficient = -mask_row * (rank_row - mean_t) / spread_t / every

    forward(0, chip_total(0))
    forward(1, chip_total(1))

    arrived(ar, 4)
    mine = s1[ours, :]
    for n in range(len(same_core)):
        mine = mine + ar[n].astype(F32)
    full[ours, :] = mine * coefficient
    full_copy = copy_to(full.at[ours], full.at[ours], chain_sem.at[6], chain_sem.at[7], other)
    full_copy.start()

    lax.fori_loop(GAP_ONE, GAP_TWO, compute, 0)

    full_copy.wait_recv()
    back = full[32:64, :].astype(BF16)
    p_high, p_low = high_low(full[0:32, :])
    g[:, 0:inner] = adapter_scale * contract(back, hid[...], 1, 0)
    right = contract(jnp.concatenate([p_high, p_low], axis=0), cot[...], 1, 0)
    g[:, inner : inner + width] = adapter_scale * (right[0:32] + right[32:64])
    g[:, inner + width :] = jnp.zeros((32, 4 * quarter - inner - width), F32)
    for r in range(nd):
        value = quarters(g[4 * r : 4 * r + 4, :], quarter)
        gf[r] = value
        gs[r] = value.astype(BF16)
    to_dp(lambda peer: gs.at[peer], lambda n: gr.at[n], 8)

    forward(2, chip_total(2) + received(0))
    forward(3, chip_total(3) + received(1))
    lax.fori_loop(GAP_TWO, chips, compute, 0)
    forward(4, chip_total(4))
    forward(5, chip_total(5))

    for copy in late:
        copy.wait()

    def own_rows(value_a, value_b, slot):
        rows = pl.ds(pl.multiple_of((i // 2) * 8, 8), 8)
        odd = lax.rem(i, 2) == 1

        def pick(ref):
            eight = ref[rows, :]
            return jnp.where(odd, eight[4:8], eight[0:4])

        pad = jnp.zeros((4, 4 * quarter - inner - width), F32)
        own[slot] = quarters(jnp.concatenate([pick(value_a), pick(value_b), pad], axis=1), quarter)

    own_rows(a, b, 0)
    own_rows(ma, mb, 1)
    own_rows(va, vb, 2)

    arrived(gr, 8)
    grad = gf[i]
    for n in range(nd - 1):
        grad = grad + gr[n].astype(F32)
    first = 0.9 * own[1] + 0.1 * grad
    second = 0.999 * own[2] + 0.001 * grad * grad
    param = own[0] - 0.004 * (first / bias_one) / (jnp.sqrt(second / bias_two) + 1e-08)
    a_send = param.astype(BF16)

    def split(value, left_ref, right_ref):
        for q in range(4):
            lo, hi = q * quarter, (q + 1) * quarter
            rows = value[4 * q : 4 * q + 4]
            if lo < inner and left_ref is not None:
                left_ref[:, lo : min(hi, inner)] = rows[:, : min(hi, inner) - lo]
            start, stop = max(lo, inner), min(hi, inner + width)
            if start < stop:
                right_ref[:, start - inner : stop - inner] = rows[:, start - lo : stop - lo]

    home = t // 2
    at_home = home == i
    split(a_send.astype(F32), None, bs)

    def home_copy():
        return copy_to(bs, bc.at[i], b_sem.at[0], b_sem.at[1], {"dp": home})

    @pl.when(jnp.logical_not(at_home))
    def _():
        home_copy().start()

    partial = None
    for q in range(4):
        cols = min(quarter, inner - q * quarter)
        if cols <= 0:
            continue
        part = contract(a_send[:, :cols], x[:, q * quarter : q * quarter + cols], 1, 1)
        part = part[4 * q : 4 * q + 4]
        partial = part if partial is None else partial + part
    xa_s[...] = jnp.concatenate([partial[:, :half_tok], partial[:, half_tok:]], axis=0)
    to_tensor(xa_s, lambda n: xa_r.at[n], 10, tensor_all)

    split(param, o_pa, o_pb)
    split(first, o_ma, o_mb)
    split(second, o_va, o_vb)

    forward(6, chip_total(6) + received(4) + received(3))
    keep[chips - 1] = chip_total(chips - 1) + received(2) + received(5)

    arrived(xa_r, 10)
    mine = xa_s[...]
    for n in range(len(tensor_all)):
        mine = mine + xa_r[n]
    xall[i] = mine
    to_dp(lambda peer: xall.at[i], lambda n: xall.at[i], 12)

    def column_copy(k):
        cols = pl.ds(128 * k, 128)
        return copy_to(
            bc.at[:, :, cols], bd, b_sem.at[2 + k], b_sem.at[10], {"tensor": 8 * core + k}
        )

    @pl.when(at_home)
    def _():
        pltpu.make_async_copy(bc.at[pl.ds(0, nd - 1)], bc.at[pl.ds(0, nd - 1)], b_sem.at[1]).wait()
        bc[i] = bs[...]
        for k in range(8):
            here = 8 * core + k == t

            @pl.when(jnp.logical_not(here))
            def _():
                column_copy(k).start()

            @pl.when(here)
            def _():
                bd[...] = bc[:, :, 128 * k : 128 * k + 128]

    keep[chips - 1] = keep[chips - 1] + received(6)

    @pl.when(2 * i + t // 8 != t)
    def _():
        pltpu.make_async_copy(bd, bd, b_sem.at[10]).wait()

    nothing = jnp.zeros((nd, 4, 128), F32)
    b_rows = bd[...]
    xall_bytes = xa_r.at[pl.ds(0, nd - 1)]
    arrived(xall_bytes, 12)
    z_high, z_low = high_low(xall[...].reshape(8 * nd, half_tok))
    z = jnp.concatenate([z_high, z_low], axis=0)
    for h in range(2):
        b_half = jnp.concatenate([nothing, b_rows] if h else [b_rows, nothing], axis=1)
        b_half = b_half.reshape(8 * nd, 128).astype(BF16)
        added = contract(z, jnp.concatenate([b_half, b_half], axis=0), 0, 0)
        rows = slice(h * half_tok, (h + 1) * half_tok)
        o_out[rows, :] = (keep[chips - 1, rows, :] + adapter_scale * added).astype(BF16)

    sent(stat_r, 0)
    chip_copy.wait_send()
    sent(ar, 4)
    full_copy.wait_send()
    sent(gr, 8)
    sent(xa_r, 10)
    sent(xall_bytes, 12)
    for s in range(chips):
        pair_copy(s).wait_send()
    for n in range(len(routes)):
        part_copy(n).wait_send()

    @pl.when(jnp.logical_not(at_home))
    def _():
        home_copy().wait_send()

    @pl.when(at_home)
    def _():
        for k in range(8):

            @pl.when(8 * core + k != t)
            def _():
                column_copy(k).wait_send()


def hand_over(*refs):
    *refs, sems = refs
    count = len(refs) // 2
    copies = [
        pltpu.make_async_copy(refs[n], refs[count + n], sems.at[n]) for n in range(count)
    ]
    for copy in copies:
        copy.start()
    for copy in copies:
        copy.wait()


def shards(
    hidden, cotangent, prompt_group_index, answer_token_mask, token_reward_order,
    source_lowdim_matrix, running_mean_source_matrix, running_variance_source_matrix,
    target_lowdim_matrix, running_mean_target_matrix, running_variance_target_matrix,
    frozen_down_weight, sampled_token_input,
):
    nd, nt = lax.axis_size("dp"), lax.axis_size("tensor")
    tokens, inner = hidden.shape
    width = cotangent.shape[1]
    rank = source_lowdim_matrix.shape[0]
    columns = frozen_down_weight.shape[1]
    rollout = sampled_token_input.shape[0]
    n_groups = tokens * nd // 8
    chips = nt // 2
    quarter = -(-(inner + width) // 512) * 128
    rows = rank // nd
    vmem, dma = pltpu.VMEM, pltpu.SemaphoreType.DMA
    i32 = jnp.int32
    scratch = [
        vmem((tokens, inner), BF16), vmem((tokens, width), BF16),
        vmem((1, tokens), i32), vmem((1, tokens), i32), vmem((1, tokens), i32),
        vmem((rank, inner), F32), vmem((rank, inner), F32), vmem((rank, inner), F32),
        vmem((rank, width), F32), vmem((rank, width), F32), vmem((rank, width), F32),
        vmem((chips, inner, 256), BF16), vmem((rollout, inner), BF16),
        vmem((8, n_groups), F32), vmem((nd - 1, 8, n_groups), F32),
        vmem((64, tokens), F32), vmem((32, tokens), F32), vmem((32, tokens), BF16),
        vmem((chips - 1, 32, tokens), BF16), vmem((64, tokens), F32),
        vmem((rank, 4 * quarter), F32), vmem((nd, 16, quarter), F32), vmem((nd, 16, quarter), BF16),
        vmem((nd - 1, 16, quarter), BF16), vmem((3, 16, quarter), F32),
        vmem((8, rollout // 2), F32), vmem((nt - 1, 8, rollout // 2), F32),
        vmem((nd, 8, rollout // 2), F32), vmem((rows, width), F32), vmem((nd, rows, width), F32),
        vmem((nd, rows, 128), F32),
        vmem((chips, rollout, 128), F32), vmem((chips, rollout, 128), BF16),
        vmem((chips, rollout, 128), BF16), vmem((7, rollout, 128), BF16),
        vmem((7, rollout, 128), BF16),
        dma((13,)), dma((chips,)), dma((chips,)), dma((chips,)), dma((7,)), dma((7,)), dma((11,)),
        dma((14,)),
    ]
    results = [((rollout, 128), BF16)] + [((rows, inner), F32)] * 3 + [((rows, width), F32)] * 3
    held = pl.pallas_call(
        functools.partial(kernel, nd, nt),
        out_shape=[vmem(shape, dtype) for shape, dtype in results],
        in_specs=[pl.BlockSpec(memory_space=pl.ANY)] * 13,
        out_specs=[pl.BlockSpec(memory_space=vmem)] * 7,
        scratch_shapes=scratch,
        compiler_params=pltpu.CompilerParams(
            collective_id=0, has_side_effects=True, vmem_limit_bytes=56 * 2**20
        ),
        name="grpo_step",
    )(
        hidden, cotangent,
        prompt_group_index.reshape(1, tokens), answer_token_mask.reshape(1, tokens),
        token_reward_order.reshape(1, tokens),
        source_lowdim_matrix, running_mean_source_matrix, running_variance_source_matrix,
        target_lowdim_matrix, running_mean_target_matrix, running_variance_target_matrix,
        frozen_down_weight, sampled_token_input,
    )
    held = [pltpu.with_memory_space_constraint(value, vmem) for value in held]
    return pl.pallas_call(
        hand_over,
        out_shape=tuple(jax.ShapeDtypeStruct(shape, dtype) for shape, dtype in results),
        in_specs=[pl.BlockSpec(memory_space=vmem)] * 7,
        out_specs=[pl.BlockSpec(memory_space=pl.ANY)] * 7,
        scratch_shapes=[dma((7,))],
        name="hand_over",
    )(*held)


def solution(mesh):
    factor = P(None, "tensor")
    placed = (
        P("dp", "tensor"), P("dp", "tensor"), P("dp"), P("dp"), P("dp"),
        factor, factor, factor, factor, factor, factor, P("tensor", "dp"), factor,
    )
    owned = P("dp", "tensor")
    return jax.shard_map(
        shards,
        mesh=mesh,
        in_specs=placed,
        out_specs=(P(None, ("dp", "tensor")), owned, owned, owned, owned, owned, owned),
        check_vma=False,
    )
```

time: 56.2 us -> 36.6 us (0.65)
  local copies, waits for them, and re-layouts: 9.84 us -> 0 us
  Pallas kernels: 45 us -> 35.8 us
    unnamed x7 -> x0, local copies, waits for them, and re-layouts: 9.84 us -> none
    pallas_call x1 -> x2, Pallas kernels: 45 us -> 35.8 us  [the longest x1 35 us: shards(): pl.pallas_call(functools.partial(kernel, nd, nt), out_shape=[vmem(shape,...]
where the time goes in v2:
time: 36.6 us; the launch traced here: 36.4 us
  Pallas kernels  35.8 us (98%)
  between operations  0.65 us (2%)
    pallas_call x1, Pallas kernels, shards(): pl.pallas_call(functools.partial(kernel, nd, nt), out_shape=[vmem(shape,...  35 us
    pallas_call x1, Pallas kernels, shards(): pl.pallas_call(hand_over, out_shape=tuple((jax.ShapeDtypeStruct(shape, dt...  0.78 us

profile of v2, /device:TPU:1, one launch (start us, length us, event | category | flops | bytes accessed | tf_op | source)
XLA Modules:
  0.0 36.4 jit_solution(15755059743932816494)
XLA Ops:
  0.6 35.0 %grpo_step.1 = (bf16[512,128]{1,0:T(8,128)(2,1)S(1)}, f32[4,3328]{1,0:T(4,128)S(1)}, f32[4,3328]{1,0:T(4,128)S(1)}, f32[4,3328]{1,0:T(4,128)S(1)}, f32[4,1024]{1...) custom-call(bf16[512,3328]{1,0:T(8,128)(2,1)} %hidden.1, bf16[512,1024]{1,0:T(8,128)(2,1)} %cotangent.1, ...), custom_call_target="tpu_custom_call" | custom-call | tf_op jit(solution)/shard_map/grpo_step/pallas_call | solution.py:452
  35.6 0.8 %hand_over.1 = (bf16[512,128]{1,0:T(8,128)(2,1)}, f32[4,3328]{1,0:T(4,128)}, f32[4,3328]{1,0:T(4,128)}, f32[4,3328]{1,0:T(4,128)}, f32[4,1024]{1,0:T(4,128)}, /*index=5*/f32[4,1024]{1,0:T(4,128)}, f32[4,1024]{1,0:T(4,128)}) custom-call(bf16[512,128]{1,0:T(8,128)(2,1)S(1)} %get-tuple-element.14.refs_0_, f32[4,3328]{1,0:T(4,128)S(1)} %get-tuple-element.15.refs_1_, ...), custom_call_target="tpu_custom_call" | custom-call | tf_op jit(solution)/shard_map/hand_over/pallas_call | solution.py:471

commit v3 on v2

v3 whole, which is shorter than its diff:
```python
import functools

import jax
import jax.numpy as jnp
from jax import lax
from jax.experimental import pallas as pl
from jax.experimental.pallas import tpu as pltpu
from jax.sharding import PartitionSpec as P

MESH = pl.DeviceIdType.MESH
F32 = jnp.float32
BF16 = jnp.bfloat16

adapter_scale = 2.0
bias_one = 1.0 - 0.9**10
bias_two = 1.0 - 0.999**10

BLOCKS = ((2, 1), (3, 1), (1, 1), (0, 1), (2, 0), (1, 0), (3, 0), (0, 0))
PARTS = ((0, ()), (1, (0,)), (2, ()), (4, ()), (5, (3,)), (6, ()), (3, (1, 2)))
GAPS = (1, 3, 3, 4, 6, 8)
SENDS = ((), (), (0,), (2,), (1, 3), (4, 5, 6))
FAR = ((2, 1), (1, 1), (3, 1), (2, 0), (0, 1), (1, 0), (3, 0))
PLANE = (
    (2, 2), (2, 1), (2, 3), (1, 2), (3, 2), (1, 1), (1, 3), (3, 1), (3, 3), (2, 0), (0, 2), (1, 0),
    (3, 0), (0, 1), (0, 3),
)


def contract(left, right, left_dim, right_dim):
    return lax.dot_general(
        left, right, (((left_dim,), (right_dim,)), ((), ())), preferred_element_type=F32
    )


def high_low(value):
    high = value.astype(BF16)
    return high, (value - high.astype(F32)).astype(BF16)


def quarters(value, width):
    return jnp.concatenate([value[:, q * width : (q + 1) * width] for q in range(4)], axis=0)


def kernel(
    nd, nt,
    hidden, cotangent, groups, mask, order, a_in, ma_in, va_in, b_in, mb_in, vb_in, weight, sampled,
    o_out, o_pa, o_ma, o_va, o_pb, o_mb, o_vb,
    hid, cot, grp, msk, odr, a, ma, va, b, mb, vb, w, x, xt,
    stat, stat_r, s1, cr, cs, ar, full, ga, gaf, gas, gar, gb, gbf, gbs, gbr, own_a, own_b,
    xa_s, xa_r, xall, bs, bc, bd, keep, give, got, part_s, part_r,
    lsem, wsem, pair_sem, got_sem, part_sem, part_rsem, b_sem, chain_sem,
):
    i = lax.axis_index("dp")
    t = lax.axis_index("tensor")
    core = lax.rem(t, 2)
    place = t // 4
    level = lax.rem(t // 2, 2)
    chips = nt // 2
    inner = hid.shape[1]
    width = cot.shape[1]
    quarter = gas.shape[2]
    quarter_b = gbs.shape[2]
    n_tok = hid.shape[0]

    def tensor_peer(dx, dz, dc):
        return lax.rem(place + dx, 4) * 4 + lax.rem(level + dz, 2) * 2 + lax.rem(core + dc, 2)

    def dp_peer(dy, dz):
        return lax.rem(i // 4 + dz, 2) * 4 + lax.rem(lax.rem(i, 4) + dy, 4)

    def plane_peer(dy, dz):
        z = lax.rem((i // 4) * 2 + level + dz, 4)
        return {
            "dp": (z // 2) * 4 + lax.rem(lax.rem(i, 4) + dy, 4),
            "tensor": place * 4 + lax.rem(z, 2) * 2 + core,
        }

    same_core = [(dx, dz, 0) for dx, dz in FAR]
    tensor_all = [(dx, dz, dc) for dx, dz in FAR for dc in (1, 0)] + [(0, 0, 1)]
    same_level = [(dx, 0, dc) for dc in (1, 0) for dx in (2, 1, 3)] + [(0, 0, 1)]

    def load(src, dst, n):
        copy = pltpu.make_async_copy(src, dst, lsem.at[n])
        copy.start()
        return copy

    b_load = load(b_in, b, 3)
    cot_load = load(cotangent, cot, 5)

    barrier = pltpu.get_barrier_semaphore()
    for dy, dz in PLANE:
        pl.semaphore_signal(barrier, inc=1, device_id=plane_peer(dy, dz), device_id_type=MESH)
    for dx, dz, dc in tensor_all:
        pl.semaphore_signal(
            barrier, inc=1, device_id={"tensor": tensor_peer(dx, dz, dc)}, device_id_type=MESH
        )

    def w_load(s):
        dx, dz = BLOCKS[s]
        block = lax.rem(place + dx, 4) * 2 + lax.rem(level + dz, 2)
        cols = pl.ds(pl.multiple_of(block * 256, 256), 256)
        pltpu.make_async_copy(weight.at[:, cols], w.at[s], wsem.at[s]).start()

    small = [load(groups, grp, 0), load(mask, msk, 1), load(order, odr, 2)]
    a_load = load(a_in, a, 4)
    pieces = (0, 1280, 2304, inner)
    hid_load = []
    for n in range(len(pieces) - 1):
        cols = pl.ds(pieces[n], pieces[n + 1] - pieces[n])
        hid_load.append(load(hidden.at[:, cols], hid.at[:, cols], 6 + n))

    x_load = load(sampled, x, 9)
    for s in range(2):
        w_load(s)

    for copy in small:
        copy.wait()
    mask_row = msk[...].astype(F32)
    rank_row = odr[...].astype(F32)
    n_groups = stat.shape[1]
    group_id = lax.broadcasted_iota(jnp.int32, (n_groups, n_tok), 0)
    member = jnp.where(group_id == grp[...], 1.0, 0.0).astype(BF16)
    row = lax.broadcasted_iota(jnp.int32, (8, n_tok), 0)
    weighted = mask_row * rank_row
    terms = jnp.where(
        row == 0, mask_row, jnp.where(row == 1, weighted, jnp.where(row == 2, weighted * rank_row, 0.0))
    )
    stat[...] = contract(terms.astype(BF16), member, 1, 1)[0:4]

    b_load.wait()
    b_high, b_low = high_low(b[...])
    cot_load.wait()
    raw = contract(jnp.concatenate([b_high, b_low], axis=0), cot[...], 1, 1)
    s1[1] = raw[0:32] + raw[32:64]


    def copy_to(src, dst, send, recv, peer):
        return pltpu.make_async_remote_copy(
            src_ref=src, dst_ref=dst, send_sem=send, recv_sem=recv, device_id=peer, device_id_type=MESH
        )

    def to_dp(src, dst, sems):
        for n, (dy, dz) in enumerate(FAR):
            peer = dp_peer(dy, dz)
            copy_to(
                src(peer), dst(n), chain_sem.at[sems], chain_sem.at[sems + 1], {"dp": peer}
            ).start()

    def to_tensor(src, dst, sems, peers):
        for n, (dx, dz, dc) in enumerate(peers):
            copy_to(
                src, dst(n), chain_sem.at[sems], chain_sem.at[sems + 1],
                {"tensor": tensor_peer(dx, dz, dc)},
            ).start()

    def arrived(ref, sems):
        pltpu.make_async_copy(ref, ref, chain_sem.at[sems + 1]).wait()

    def sent(ref, sems):
        pltpu.make_async_copy(ref, ref, chain_sem.at[sems]).wait()

    other = {"tensor": tensor_peer(0, 0, 1)}
    theirs = pl.ds(pl.multiple_of(16 - 16 * core, 16), 16)
    ours = pl.ds(pl.multiple_of(16 * core, 16), 16)

    def chip_copy(n):
        return copy_to(
            s1.at[n, theirs], cr.at[n], chain_sem.at[12 + 2 * n], chain_sem.at[13 + 2 * n], other
        )

    def full_copy(n):
        return copy_to(
            full.at[n, ours], full.at[n, ours], chain_sem.at[16 + 2 * n], chain_sem.at[17 + 2 * n], other
        )

    def to_chips(n):
        chip_copy(n).wait_recv()
        chip_sum = s1[n, ours, :] + cr[n]
        s1[n, ours, :] = chip_sum
        cs[n] = chip_sum.astype(BF16)
        to_tensor(cs.at[n], lambda m: ar.at[n, m], 2 + 2 * n, same_core)

    def from_chips(n):
        arrived(ar.at[n], 2 + 2 * n)
        mine = s1[n, ours, :]
        for m in range(len(same_core)):
            mine = mine + ar[n, m].astype(F32)
        full[n, ours, :] = mine
        full_copy(n).start()

    pl.semaphore_wait(barrier, len(tensor_all) + len(PLANE))
    chip_copy(1).start()

    to_dp(lambda peer: stat, lambda n: stat_r.at[n], 0)
    to_chips(1)

    a_load.wait()
    a_half = a[...].astype(BF16)
    total = None
    for n, copy in enumerate(hid_load):
        copy.wait()
        cols = slice(pieces[n], pieces[n + 1])
        part = contract(a_half[:, cols], hid[:, cols], 1, 1)
        total = part if total is None else total + part
    s1[0] = total
    chip_copy(0).start()
    for s in range(2, 4):
        w_load(s)
    late = [load(ma_in, ma, 10), load(va_in, va, 11), load(mb_in, mb, 12), load(vb_in, vb, 13)]
    for s in range(4, chips):
        w_load(s)

    def pair_copy(s):
        return copy_to(give.at[s], got.at[s], pair_sem.at[s], got_sem.at[s], other)

    def compute(s, carry):
        pltpu.make_async_copy(weight.at[:, pl.ds(0, 256)], w.at[s], wsem.at[s]).wait()
        block = contract(x[...], w[s], 1, 0)
        first, second = block[:, :128], block[:, 128:]
        keep[s] = jnp.where(core == 0, first, second)
        give[s] = jnp.where(core == 0, second, first).astype(BF16)
        pair_copy(s).start()
        return carry

    def chip_total(s):
        pair_copy(s).wait_recv()
        return keep[s] + got[s].astype(F32)

    ahead = {"tensor": tensor_peer(1, 0, 0)}
    behind = {"tensor": tensor_peer(3, 0, 0)}
    across = {"tensor": tensor_peer(0, 1, 0)}
    routes = (behind, behind, ahead, ahead, ahead, behind, across)

    def part_copy(n):
        return copy_to(part_s.at[n], part_r.at[n], part_sem.at[n], part_rsem.at[n], routes[n])

    def forward(n, value):
        part_s[n] = value.astype(BF16)
        part_copy(n).start()

    def received(n):
        part_copy(n).wait_recv()
        return part_r[n].astype(F32)

    def run(gap):
        first = GAPS[gap - 1] if gap else 0
        if first == 0 and GAPS[gap]:
            x_load.wait()
        if first < GAPS[gap]:
            lax.fori_loop(first, GAPS[gap], compute, 0)
        for n in SENDS[gap]:
            block, parts = PARTS[n]
            value = chip_total(block)
            for m in parts:
                value = value + received(m)
            forward(n, value)

    run(0)
    to_chips(0)
    run(1)

    from_chips(1)
    arrived(stat_r, 0)
    stats = stat[...]
    for d in range(nd - 1):
        stats = stats + stat_r[d]
    counts, sums, squares = stats[0:1], stats[1:2], stats[2:3]
    safe = jnp.maximum(counts, 1.0)
    mean = sums / safe
    spread = jnp.maximum(jnp.sqrt(jnp.maximum(squares / safe - mean * mean, 0.0)), 1.0)
    every = jnp.maximum(jnp.sum(counts, axis=1, keepdims=True), 1.0)
    table = jnp.zeros((8, n_groups), F32)
    row_g = lax.broadcasted_iota(jnp.int32, (8, n_groups), 0)
    for base, value in ((0, mean), (3, spread)):
        rest = value
        for n in range(3):
            term = rest.astype(BF16).astype(F32)
            table = jnp.where(row_g == base + n, term, table)
            rest = rest - term
    looked = contract(table.astype(BF16), member, 1, 0)
    mean_t = (looked[0:1] + looked[1:2]) + looked[2:3]
    spread_t = (looked[3:4] + looked[4:5]) + looked[5:6]
    coefficient = -mask_row * (rank_row - mean_t) / spread_t / every

    full_copy(1).wait_recv()
    ga[:, 0:inner] = adapter_scale * contract((full[1] * coefficient).astype(BF16), hid[...], 1, 0)
    ga[:, inner:] = jnp.zeros((32, 4 * quarter - inner), F32)
    for r in range(nd):
        value = quarters(ga[4 * r : 4 * r + 4, :], quarter)
        gaf[r] = value
        gas[r] = value.astype(BF16)
    to_dp(lambda peer: gas.at[peer], lambda n: gar.at[n], 6)

    from_chips(0)
    run(2)
    run(3)

    full_copy(0).wait_recv()
    p_high, p_low = high_low(full[0] * coefficient)
    right = contract(jnp.concatenate([p_high, p_low], axis=0), cot[...], 1, 0)
    gb[...] = adapter_scale * (right[0:32] + right[32:64])
    for r in range(nd):
        value = quarters(gb[4 * r : 4 * r + 4, :], quarter_b)
        gbf[r] = value
        gbs[r] = value.astype(BF16)
    to_dp(lambda peer: gbs.at[peer], lambda n: gbr.at[n], 20)

    for copy in late:
        copy.wait()

    def own_rows(ref, quarter):
        rows = pl.ds(pl.multiple_of((i // 2) * 8, 8), 8)
        eight = ref[rows, :]
        four = jnp.where(lax.rem(i, 2) == 1, eight[4:8], eight[0:4])
        pad = 4 * quarter - four.shape[1]
        if pad:
            four = jnp.concatenate([four, jnp.zeros((4, pad), F32)], axis=1)
        return quarters(four, quarter)

    for n, (ref_a, ref_b) in enumerate(((a, b), (ma, mb), (va, vb))):
        own_a[n] = own_rows(ref_a, quarter)
        own_b[n] = own_rows(ref_b, quarter_b)

    run(4)

    def adam(own, grad, received_grads):
        for n in range(nd - 1):
            grad = grad + received_grads[n].astype(F32)
        first = 0.9 * own[1] + 0.1 * grad
        second = 0.999 * own[2] + 0.001 * grad * grad
        param = own[0] - 0.004 * (first / bias_one) / (jnp.sqrt(second / bias_two) + 1e-08)
        return param, first, second

    def split(value, ref, quarter):
        columns = ref.shape[1]
        for q in range(4):
            lo, hi = q * quarter, min((q + 1) * quarter, columns)
            ref[:, lo:hi] = value[4 * q : 4 * q + 4, : hi - lo]

    for n in range(inner // 256):
        xt[256 * n : 256 * (n + 1), :] = x[:, 256 * n : 256 * (n + 1)].T
    arrived(gar, 6)
    adam_a = adam(own_a, gaf[i], gar)
    a_send = adam_a[0].astype(BF16)
    partial = None
    for q in range(4):
        lo, hi = q * quarter, min((q + 1) * quarter, inner)
        part = contract(a_send[:, : hi - lo], xt[lo:hi, :], 1, 0)
        part = part[4 * q : 4 * q + 4]
        partial = part if partial is None else partial + part
    partial = quarters(partial, n_tok // 4)
    xa_s[...] = partial.astype(BF16)
    to_tensor(xa_s, lambda n: xa_r.at[n], 8, same_level)

    arrived(gbr, 20)
    adam_b = adam(own_b, gbf[i], gbr)
    home = t // 2
    at_home = home == i
    split(adam_b[0].astype(BF16).astype(F32), bs, quarter_b)

    def home_copy():
        return copy_to(bs, bc.at[i], b_sem.at[0], b_sem.at[1], {"dp": home})

    @pl.when(jnp.logical_not(at_home))
    def _():
        home_copy().start()

    for value, ref in zip(adam_a, (o_pa, o_ma, o_va)):
        split(value, ref, quarter)
    for value, ref in zip(adam_b, (o_pb, o_mb, o_vb)):
        split(value, ref, quarter_b)

    run(5)

    arrived(xa_r, 8)
    mine = partial
    for n in range(len(same_level)):
        mine = mine + xa_r[n].astype(F32)
    slot = level * nd + i
    xall[slot] = mine.astype(BF16)
    for dy, dz in PLANE:
        copy_to(
            xall.at[slot], xall.at[slot], chain_sem.at[10], chain_sem.at[11], plane_peer(dy, dz)
        ).start()

    def column_copy(k):
        cols = pl.ds(128 * k, 128)
        return copy_to(
            bc.at[:, :, cols], bd, b_sem.at[2 + k], b_sem.at[10], {"tensor": 8 * core + k}
        )

    @pl.when(at_home)
    def _():
        pltpu.make_async_copy(bc.at[pl.ds(0, nd - 1)], bc.at[pl.ds(0, nd - 1)], b_sem.at[1]).wait()
        bc[i] = bs[...]
        for k in range(8):
            here = 8 * core + k == t

            @pl.when(jnp.logical_not(here))
            def _():
                column_copy(k).start()

            @pl.when(here)
            def _():
                bd[...] = bc[:, :, 128 * k : 128 * k + 128]

    keep[chips - 1] = chip_total(chips - 1) + received(4) + received(5) + received(6)

    @pl.when(2 * i + t // 8 != t)
    def _():
        pltpu.make_async_copy(bd, bd, b_sem.at[10]).wait()

    b_rows = bd[...]
    b_rows = jnp.concatenate([b_rows] * 4, axis=1).reshape(16 * nd, 128)
    row_b = lax.rem(lax.broadcasted_iota(jnp.int32, (16 * nd, 128), 0), 16) // 4
    b_parts = [jnp.where(row_b == q, b_rows, 0.0).astype(BF16) for q in range(4)]
    xall_bytes = xall.at[pl.ds(0, len(PLANE))]
    arrived(xall_bytes, 10)
    z = xall[...].reshape(32 * nd, n_tok // 4)
    for q in range(4):
        added = contract(z, jnp.concatenate([b_parts[q], b_parts[q]], axis=0), 0, 0)
        rows = slice(q * (n_tok // 4), (q + 1) * (n_tok // 4))
        o_out[rows, :] = (keep[chips - 1, rows, :] + adapter_scale * added).astype(BF16)

    sent(stat_r, 0)
    for n in range(2):
        chip_copy(n).wait_send()
        sent(ar.at[n], 2 + 2 * n)
        full_copy(n).wait_send()
    sent(gar, 6)
    sent(gbr, 20)
    sent(xa_r, 8)
    sent(xall_bytes, 10)
    for s in range(chips):
        pair_copy(s).wait_send()
    for n in range(len(routes)):
        part_copy(n).wait_send()

    @pl.when(jnp.logical_not(at_home))
    def _():
        home_copy().wait_send()

    @pl.when(at_home)
    def _():
        for k in range(8):

            @pl.when(8 * core + k != t)
            def _():
                column_copy(k).wait_send()


def hand_over(*refs):
    *refs, sems = refs
    count = len(refs) // 2
    copies = [
        pltpu.make_async_copy(refs[n], refs[count + n], sems.at[n]) for n in range(count)
    ]
    for copy in copies:
        copy.start()
    for copy in copies:
        copy.wait()


def shards(
    hidden, cotangent, prompt_group_index, answer_token_mask, token_reward_order,
    source_lowdim_matrix, running_mean_source_matrix, running_variance_source_matrix,
    target_lowdim_matrix, running_mean_target_matrix, running_variance_target_matrix,
    frozen_down_weight, sampled_token_input,
):
    nd, nt = lax.axis_size("dp"), lax.axis_size("tensor")
    tokens, inner = hidden.shape
    width = cotangent.shape[1]
    rank = source_lowdim_matrix.shape[0]
    columns = frozen_down_weight.shape[1]
    rollout = sampled_token_input.shape[0]
    n_groups = tokens * nd // 8
    chips = nt // 2
    quarter, quarter_b = -(-inner // 512) * 128, -(-width // 512) * 128
    rows = rank // nd
    vmem, dma = pltpu.VMEM, pltpu.SemaphoreType.DMA
    i32 = jnp.int32
    scratch = [
        vmem((tokens, inner), BF16), vmem((tokens, width), BF16),
        vmem((1, tokens), i32), vmem((1, tokens), i32), vmem((1, tokens), i32),
        vmem((rank, inner), F32), vmem((rank, inner), F32), vmem((rank, inner), F32),
        vmem((rank, width), F32), vmem((rank, width), F32), vmem((rank, width), F32),
        vmem((chips, inner, 256), BF16), vmem((rollout, inner), BF16),
        vmem((inner, rollout), BF16),
        vmem((4, n_groups), F32), vmem((nd - 1, 4, n_groups), F32),
        vmem((2, 32, tokens), F32), vmem((2, 16, tokens), F32), vmem((2, 16, tokens), BF16),
        vmem((2, chips - 1, 16, tokens), BF16), vmem((2, 32, tokens), F32),
        vmem((rank, 4 * quarter), F32), vmem((nd, 16, quarter), F32), vmem((nd, 16, quarter), BF16),
        vmem((nd - 1, 16, quarter), BF16),
        vmem((rank, 4 * quarter_b), F32), vmem((nd, 16, quarter_b), F32),
        vmem((nd, 16, quarter_b), BF16), vmem((nd - 1, 16, quarter_b), BF16),
        vmem((3, 16, quarter), F32), vmem((3, 16, quarter_b), F32),
        vmem((16, rollout // 4), BF16), vmem((chips - 1, 16, rollout // 4), BF16),
        vmem((2 * nd, 16, rollout // 4), BF16), vmem((rows, width), F32), vmem((nd, rows, width), F32),
        vmem((nd, rows, 128), F32),
        vmem((chips, rollout, 128), F32), vmem((chips, rollout, 128), BF16),
        vmem((chips, rollout, 128), BF16), vmem((7, rollout, 128), BF16),
        vmem((7, rollout, 128), BF16),
        dma((14,)), dma((chips,)), dma((chips,)), dma((chips,)), dma((7,)), dma((7,)), dma((11,)),
        dma((22,)),
    ]
    results = [((rollout, 128), BF16)] + [((rows, inner), F32)] * 3 + [((rows, width), F32)] * 3
    held = pl.pallas_call(
        functools.partial(kernel, nd, nt),
        out_shape=[vmem(shape, dtype) for shape, dtype in results],
        in_specs=[pl.BlockSpec(memory_space=pl.ANY)] * 13,
        out_specs=[pl.BlockSpec(memory_space=vmem)] * 7,
        scratch_shapes=scratch,
        compiler_params=pltpu.CompilerParams(
            collective_id=0, has_side_effects=True, vmem_limit_bytes=56 * 2**20
        ),
        name="grpo_step",
    )(
        hidden, cotangent,
        prompt_group_index.reshape(1, tokens), answer_token_mask.reshape(1, tokens),
        token_reward_order.reshape(1, tokens),
        source_lowdim_matrix, running_mean_source_matrix, running_variance_source_matrix,
        target_lowdim_matrix, running_mean_target_matrix, running_variance_target_matrix,
        frozen_down_weight, sampled_token_input,
    )
    held = [pltpu.with_memory_space_constraint(value, vmem) for value in held]
    return pl.pallas_call(
        hand_over,
        out_shape=tuple(jax.ShapeDtypeStruct(shape, dtype) for shape, dtype in results),
        in_specs=[pl.BlockSpec(memory_space=vmem)] * 7,
        out_specs=[pl.BlockSpec(memory_space=pl.ANY)] * 7,
        scratch_shapes=[dma((7,))],
        name="hand_over",
    )(*held)


def solution(mesh):
    factor = P(None, "tensor")
    placed = (
        P("dp", "tensor"), P("dp", "tensor"), P("dp"), P("dp"), P("dp"),
        factor, factor, factor, factor, factor, factor, P("tensor", "dp"), factor,
    )
    owned = P("dp", "tensor")
    return jax.shard_map(
        shards,
        mesh=mesh,
        in_specs=placed,
        out_specs=(P(None, ("dp", "tensor")), owned, owned, owned, owned, owned, owned),
        check_vma=False,
    )
```

time: 36.6 us -> 33.3 us (0.910)
  Pallas kernels: 35.8 us -> 32.6 us
    pallas_call x1, Pallas kernels: 35 us -> 31.8 us  [shards(): pl.pallas_call(functools.partial(kernel, nd, nt), out_shape=[vmem(shape,...]
where the time goes in v3:
time: 33.3 us; the launch traced here: 33.2 us
  Pallas kernels  32.6 us (98%)
  between operations  0.65 us (2%)
    pallas_call x1, Pallas kernels, shards(): pl.pallas_call(functools.partial(kernel, nd, nt), out_shape=[vmem(shape,...  31.8 us
    pallas_call x1, Pallas kernels, shards(): pl.pallas_call(hand_over, out_shape=tuple((jax.ShapeDtypeStruct(shape, dt...  0.78 us

profile of v3, /device:TPU:1, one launch (start us, length us, event | category | flops | bytes accessed | tf_op | source)
XLA Modules:
  0.0 33.2 jit_solution(8729823128228266636)
XLA Ops:
  0.6 31.8 %grpo_step.1 = (bf16[512,128]{1,0:T(8,128)(2,1)S(1)}, f32[4,3328]{1,0:T(4,128)S(1)}, f32[4,3328]{1,0:T(4,128)S(1)}, f32[4,3328]{1,0:T(4,128)S(1)}, f32[4,1024]{1...) custom-call(bf16[512,3328]{1,0:T(8,128)(2,1)} %hidden.1, bf16[512,1024]{1,0:T(8,128)(2,1)} %cotangent.1, ...), custom_call_target="tpu_custom_call" | custom-call | tf_op jit(solution)/shard_map/grpo_step/pallas_call | solution.py:507
  32.5 0.8 %hand_over.1 = (bf16[512,128]{1,0:T(8,128)(2,1)}, f32[4,3328]{1,0:T(4,128)}, f32[4,3328]{1,0:T(4,128)}, f32[4,3328]{1,0:T(4,128)}, f32[4,1024]{1,0:T(4,128)}, /*index=5*/f32[4,1024]{1,0:T(4,128)}, f32[4,1024]{1,0:T(4,128)}) custom-call(bf16[512,128]{1,0:T(8,128)(2,1)S(1)} %get-tuple-element.14.refs_0_, f32[4,3328]{1,0:T(4,128)S(1)} %get-tuple-element.15.refs_1_, ...), custom_call_target="tpu_custom_call" | custom-call | tf_op jit(solution)/shard_map/hand_over/pallas_call | solution.py:526

commit v4 on v3

--- a/solution.py
+++ b/solution.py
@@ -1,4 +1,5 @@
 import functools
+import math
 
 import jax
 import jax.numpy as jnp
@@ -18,7 +19,8 @@
 BLOCKS = ((2, 1), (3, 1), (1, 1), (0, 1), (2, 0), (1, 0), (3, 0), (0, 0))
 PARTS = ((0, ()), (1, (0,)), (2, ()), (4, ()), (5, (3,)), (6, ()), (3, (1, 2)))
 GAPS = (1, 3, 3, 4, 6, 8)
-SENDS = ((), (), (0,), (2,), (1, 3), (4, 5, 6))
+ARRIVALS = ((0, 1), (1, 3), (3, 4), (4, 7))
+SENDS = ((), (), (0,), (2,), (3, 1), (6, 4, 5))
 FAR = ((2, 1), (1, 1), (3, 1), (2, 0), (0, 1), (1, 0), (3, 0))
 PLANE = (
     (2, 2), (2, 1), (2, 3), (1, 2), (3, 2), (1, 1), (1, 3), (3, 1), (3, 3), (2, 0), (0, 2), (1, 0),
@@ -45,10 +47,10 @@
     nd, nt,
     hidden, cotangent, groups, mask, order, a_in, ma_in, va_in, b_in, mb_in, vb_in, weight, sampled,
     o_out, o_pa, o_ma, o_va, o_pb, o_mb, o_vb,
-    hid, cot, grp, msk, odr, a, ma, va, b, mb, vb, w, x, xt,
+    hid, cot, ints, a, mva, b, mvb, w, x, xt,
     stat, stat_r, s1, cr, cs, ar, full, ga, gaf, gas, gar, gb, gbf, gbs, gbr, own_a, own_b,
     xa_s, xa_r, xall, bs, bc, bd, keep, give, got, part_s, part_r,
-    lsem, wsem, pair_sem, got_sem, part_sem, part_rsem, b_sem, chain_sem,
+    lsem, out_sem, in_sem,
 ):
     i = lax.axis_index("dp")
     t = lax.axis_index("tensor")
@@ -79,13 +81,16 @@
     tensor_all = [(dx, dz, dc) for dx, dz in FAR for dc in (1, 0)] + [(0, 0, 1)]
     same_level = [(dx, 0, dc) for dc in (1, 0) for dx in (2, 1, 3)] + [(0, 0, 1)]
 
+    def landed(ref, sem):
+        pltpu.make_async_copy(ref, ref, sem).wait()
+
     def load(src, dst, n):
         copy = pltpu.make_async_copy(src, dst, lsem.at[n])
         copy.start()
         return copy
 
-    b_load = load(b_in, b, 3)
-    cot_load = load(cotangent, cot, 5)
+    b_load = load(b_in, b, 1)
+    cot_load = load(cotangent, cot, 2)
 
     barrier = pltpu.get_barrier_semaphore()
     for dy, dz in PLANE:
@@ -99,27 +104,27 @@
         dx, dz = BLOCKS[s]
         block = lax.rem(place + dx, 4) * 2 + lax.rem(level + dz, 2)
         cols = pl.ds(pl.multiple_of(block * 256, 256), 256)
-        pltpu.make_async_copy(weight.at[:, cols], w.at[s], wsem.at[s]).start()
-
-    small = [load(groups, grp, 0), load(mask, msk, 1), load(order, odr, 2)]
-    a_load = load(a_in, a, 4)
+        load(weight.at[:, cols], w.at[s], 10 + s)
+
+    for n, source in enumerate((groups, mask, order)):
+        load(source, ints.at[n], 0)
+    a_load = load(a_in, a, 3)
     pieces = (0, 1280, 2304, inner)
     hid_load = []
     for n in range(len(pieces) - 1):
         cols = pl.ds(pieces[n], pieces[n + 1] - pieces[n])
-        hid_load.append(load(hidden.at[:, cols], hid.at[:, cols], 6 + n))
-
-    x_load = load(sampled, x, 9)
+        hid_load.append(load(hidden.at[:, cols], hid.at[:, cols], 4 + n))
+
+    x_load = load(sampled, x, 7)
     for s in range(2):
         w_load(s)
 
-    for copy in small:
-        copy.wait()
-    mask_row = msk[...].astype(F32)
-    rank_row = odr[...].astype(F32)
+    landed(ints, lsem.at[0])
+    mask_row = ints[1].astype(F32)
+    rank_row = ints[2].astype(F32)
     n_groups = stat.shape[1]
     group_id = lax.broadcasted_iota(jnp.int32, (n_groups, n_tok), 0)
-    member = jnp.where(group_id == grp[...], 1.0, 0.0).astype(BF16)
+    member = jnp.where(group_id == ints[0], 1.0, 0.0).astype(BF16)
     row = lax.broadcasted_iota(jnp.int32, (8, n_tok), 0)
     weighted = mask_row * rank_row
     terms = jnp.where(
@@ -133,64 +138,47 @@
     raw = contract(jnp.concatenate([b_high, b_low], axis=0), cot[...], 1, 1)
     s1[1] = raw[0:32] + raw[32:64]
 
-
     def copy_to(src, dst, send, recv, peer):
         return pltpu.make_async_remote_copy(
             src_ref=src, dst_ref=dst, send_sem=send, recv_sem=recv, device_id=peer, device_id_type=MESH
         )
 
-    def to_dp(src, dst, sems):
-        for n, (dy, dz) in enumerate(FAR):
+    pushed = []
+
+    def push(src, dst, n, peer, times=1):
+        pushed.append(times * math.prod(src.shape) * jnp.dtype(src.dtype).itemsize)
+        return copy_to(src, dst, out_sem.at[0], in_sem.at[n], peer)
+
+    def to_dp(src, dst, n):
+        for m, (dy, dz) in enumerate(FAR):
             peer = dp_peer(dy, dz)
-            copy_to(
-                src(peer), dst(n), chain_sem.at[sems], chain_sem.at[sems + 1], {"dp": peer}
-            ).start()
-
-    def to_tensor(src, dst, sems, peers):
-        for n, (dx, dz, dc) in enumerate(peers):
-            copy_to(
-                src, dst(n), chain_sem.at[sems], chain_sem.at[sems + 1],
-                {"tensor": tensor_peer(dx, dz, dc)},
-            ).start()
-
-    def arrived(ref, sems):
-        pltpu.make_async_copy(ref, ref, chain_sem.at[sems + 1]).wait()
-
-    def sent(ref, sems):
-        pltpu.make_async_copy(ref, ref, chain_sem.at[sems]).wait()
+            push(src(peer), dst(m), n, {"dp": peer}).start()
+
+    def to_tensor(src, dst, n, peers):
+        for m, (dx, dz, dc) in enumerate(peers):
+            push(src, dst(m), n, {"tensor": tensor_peer(dx, dz, dc)}).start()
 
     other = {"tensor": tensor_peer(0, 0, 1)}
     theirs = pl.ds(pl.multiple_of(16 - 16 * core, 16), 16)
     ours = pl.ds(pl.multiple_of(16 * core, 16), 16)
 
-    def chip_copy(n):
-        return copy_to(
-            s1.at[n, theirs], cr.at[n], chain_sem.at[12 + 2 * n], chain_sem.at[13 + 2 * n], other
-        )
-
-    def full_copy(n):
-        return copy_to(
-            full.at[n, ours], full.at[n, ours], chain_sem.at[16 + 2 * n], chain_sem.at[17 + 2 * n], other
-        )
-
     def to_chips(n):
-        chip_copy(n).wait_recv()
+        landed(cr.at[n], in_sem.at[3 + n])
         chip_sum = s1[n, ours, :] + cr[n]
         s1[n, ours, :] = chip_sum
         cs[n] = chip_sum.astype(BF16)
-        to_tensor(cs.at[n], lambda m: ar.at[n, m], 2 + 2 * n, same_core)
+        to_tensor(cs.at[n], lambda m: ar.at[n, m], 1 + n, same_core)
 
     def from_chips(n):
-        arrived(ar.at[n], 2 + 2 * n)
+        landed(ar.at[n], in_sem.at[1 + n])
         mine = s1[n, ours, :]
         for m in range(len(same_core)):
             mine = mine + ar[n, m].astype(F32)
         full[n, ours, :] = mine
-        full_copy(n).start()
+        push(full.at[n, ours], full.at[n, ours], 5 + n, other).start()
 
     pl.semaphore_wait(barrier, len(tensor_all) + len(PLANE))
-    chip_copy(1).start()
-
+    push(s1.at[1, theirs], cr.at[1], 4, other).start()
     to_dp(lambda peer: stat, lambda n: stat_r.at[n], 0)
     to_chips(1)
 
@@ -203,27 +191,37 @@
         part = contract(a_half[:, cols], hid[:, cols], 1, 1)
         total = part if total is None else total + part
     s1[0] = total
-    chip_copy(0).start()
+    push(s1.at[0, theirs], cr.at[0], 3, other).start()
     for s in range(2, 4):
         w_load(s)
-    late = [load(ma_in, ma, 10), load(va_in, va, 11), load(mb_in, mb, 12), load(vb_in, vb, 13)]
+    for n, (source_a, source_b) in enumerate(((ma_in, mb_in), (va_in, vb_in))):
+        load(source_a, mva.at[n], 8)
+        load(source_b, mvb.at[n], 9)
     for s in range(4, chips):
         w_load(s)
 
-    def pair_copy(s):
-        return copy_to(give.at[s], got.at[s], pair_sem.at[s], got_sem.at[s], other)
-
-    def compute(s, carry):
-        pltpu.make_async_copy(weight.at[:, pl.ds(0, 256)], w.at[s], wsem.at[s]).wait()
-        block = contract(x[...], w[s], 1, 0)
-        first, second = block[:, :128], block[:, 128:]
-        keep[s] = jnp.where(core == 0, first, second)
-        give[s] = jnp.where(core == 0, second, first).astype(BF16)
-        pair_copy(s).start()
-        return carry
+    taken = set()
+
+    def compute(lo, hi):
+        def body(s, carry):
+            landed(w.at[s], lsem.at[10 + s])
+            block = contract(x[...], w[s], 1, 0)
+            first, second = block[:, :128], block[:, 128:]
+            keep[s] = jnp.where(core == 0, first, second)
+            give[s] = jnp.where(core == 0, second, first).astype(BF16)
+            copy_to(give.at[s], got.at[s], out_sem.at[0], in_sem.at[13 + s], other).start()
+            return carry
+
+        lax.fori_loop(lo, hi, body, 0)
+        pushed.append((hi - lo) * math.prod(give.shape[1:]) * 2)
+
+    def once(key, ref, sem):
+        if key not in taken:
+            landed(ref, sem)
+        taken.add(key)
 
     def chip_total(s):
-        pair_copy(s).wait_recv()
+        landed(got.at[s], in_sem.at[13 + s])
         return keep[s] + got[s].astype(F32)
 
     ahead = {"tensor": tensor_peer(1, 0, 0)}
@@ -231,23 +229,25 @@
     across = {"tensor": tensor_peer(0, 1, 0)}
     routes = (behind, behind, ahead, ahead, ahead, behind, across)
 
-    def part_copy(n):
-        return copy_to(part_s.at[n], part_r.at[n], part_sem.at[n], part_rsem.at[n], routes[n])
+    def arrival(n):
+        return [lo <= n < hi for lo, hi in ARRIVALS].index(True)
 
     def forward(n, value):
         part_s[n] = value.astype(BF16)
-        part_copy(n).start()
+        push(part_s.at[n], part_r.at[n], 21 + arrival(n), routes[n]).start()
 
     def received(n):
-        part_copy(n).wait_recv()
+        m = arrival(n)
+        lo, hi = ARRIVALS[m]
+        once(("part", m), part_r.at[pl.ds(lo, hi - lo)], in_sem.at[21 + m])
         return part_r[n].astype(F32)
 
     def run(gap):
         first = GAPS[gap - 1] if gap else 0
-        if first == 0 and GAPS[gap]:
-            x_load.wait()
         if first < GAPS[gap]:
-            lax.fori_loop(first, GAPS[gap], compute, 0)
+            if first == 0:
+                x_load.wait()
+            compute(first, GAPS[gap])
         for n in SENDS[gap]:
             block, parts = PARTS[n]
             value = chip_total(block)
@@ -260,7 +260,7 @@
     run(1)
 
     from_chips(1)
-    arrived(stat_r, 0)
+    landed(stat_r, in_sem.at[0])
     stats = stat[...]
     for d in range(nd - 1):
         stats = stats + stat_r[d]
@@ -282,20 +282,20 @@
     spread_t = (looked[3:4] + looked[4:5]) + looked[5:6]
     coefficient = -mask_row * (rank_row - mean_t) / spread_t / every
 
-    full_copy(1).wait_recv()
+    landed(full.at[1, theirs], in_sem.at[6])
     ga[:, 0:inner] = adapter_scale * contract((full[1] * coefficient).astype(BF16), hid[...], 1, 0)
     ga[:, inner:] = jnp.zeros((32, 4 * quarter - inner), F32)
     for r in range(nd):
         value = quarters(ga[4 * r : 4 * r + 4, :], quarter)
         gaf[r] = value
         gas[r] = value.astype(BF16)
-    to_dp(lambda peer: gas.at[peer], lambda n: gar.at[n], 6)
+    to_dp(lambda peer: gas.at[peer], lambda n: gar.at[n], 7)
 
     from_chips(0)
     run(2)
     run(3)
 
-    full_copy(0).wait_recv()
+    landed(full.at[0, theirs], in_sem.at[5])
     p_high, p_low = high_low(full[0] * coefficient)
     right = contract(jnp.concatenate([p_high, p_low], axis=0), cot[...], 1, 0)
     gb[...] = adapter_scale * (right[0:32] + right[32:64])
@@ -303,10 +303,10 @@
         value = quarters(gb[4 * r : 4 * r + 4, :], quarter_b)
         gbf[r] = value
         gbs[r] = value.astype(BF16)
-    to_dp(lambda peer: gbs.at[peer], lambda n: gbr.at[n], 20)
-
-    for copy in late:
-        copy.wait()
+    to_dp(lambda peer: gbs.at[peer], lambda n: gbr.at[n], 8)
+
+    landed(mva, lsem.at[8])
+    landed(mvb, lsem.at[9])
 
     def own_rows(ref, quarter):
         rows = pl.ds(pl.multiple_of((i // 2) * 8, 8), 8)
@@ -317,9 +317,9 @@
             four = jnp.concatenate([four, jnp.zeros((4, pad), F32)], axis=1)
         return quarters(four, quarter)
 
-    for n, (ref_a, ref_b) in enumerate(((a, b), (ma, mb), (va, vb))):
-        own_a[n] = own_rows(ref_a, quarter)
-        own_b[n] = own_rows(ref_b, quarter_b)
+    for n in range(3):
+        own_a[n] = own_rows(a if n == 0 else mva.at[n - 1], quarter)
+        own_b[n] = own_rows(b if n == 0 else mvb.at[n - 1], quarter_b)
 
     run(4)
 
@@ -339,7 +339,7 @@
 
     for n in range(inner // 256):
         xt[256 * n : 256 * (n + 1), :] = x[:, 256 * n : 256 * (n + 1)].T
-    arrived(gar, 6)
+    landed(gar, in_sem.at[7])
     adam_a = adam(own_a, gaf[i], gar)
     a_send = adam_a[0].astype(BF16)
     partial = None
@@ -350,16 +350,16 @@
         partial = part if partial is None else partial + part
     partial = quarters(partial, n_tok // 4)
     xa_s[...] = partial.astype(BF16)
-    to_tensor(xa_s, lambda n: xa_r.at[n], 8, same_level)
-
-    arrived(gbr, 20)
+    to_tensor(xa_s, lambda n: xa_r.at[n], 9, same_level)
+
+    landed(gbr, in_sem.at[8])
     adam_b = adam(own_b, gbf[i], gbr)
     home = t // 2
     at_home = home == i
     split(adam_b[0].astype(BF16).astype(F32), bs, quarter_b)
 
     def home_copy():
-        return copy_to(bs, bc.at[i], b_sem.at[0], b_sem.at[1], {"dp": home})
+        return copy_to(bs, bc.at[i], out_sem.at[1], in_sem.at[11], {"dp": home})
 
     @pl.when(jnp.logical_not(at_home))
     def _():
@@ -372,26 +372,24 @@
 
     run(5)
 
-    arrived(xa_r, 8)
+    landed(xa_r, in_sem.at[9])
     mine = partial
     for n in range(len(same_level)):
         mine = mine + xa_r[n].astype(F32)
     slot = level * nd + i
     xall[slot] = mine.astype(BF16)
     for dy, dz in PLANE:
-        copy_to(
-            xall.at[slot], xall.at[slot], chain_sem.at[10], chain_sem.at[11], plane_peer(dy, dz)
-        ).start()
+        push(xall.at[slot], xall.at[slot], 10, plane_peer(dy, dz)).start()
 
     def column_copy(k):
         cols = pl.ds(128 * k, 128)
         return copy_to(
-            bc.at[:, :, cols], bd, b_sem.at[2 + k], b_sem.at[10], {"tensor": 8 * core + k}
+            bc.at[:, :, cols], bd, out_sem.at[2], in_sem.at[12], {"tensor": 8 * core + k}
         )
 
     @pl.when(at_home)
     def _():
-        pltpu.make_async_copy(bc.at[pl.ds(0, nd - 1)], bc.at[pl.ds(0, nd - 1)], b_sem.at[1]).wait()
+        landed(bc.at[pl.ds(0, nd - 1)], in_sem.at[11])
         bc[i] = bs[...]
         for k in range(8):
             here = 8 * core + k == t
@@ -408,33 +406,24 @@
 
     @pl.when(2 * i + t // 8 != t)
     def _():
-        pltpu.make_async_copy(bd, bd, b_sem.at[10]).wait()
+        landed(bd, in_sem.at[12])
 
     b_rows = bd[...]
     b_rows = jnp.concatenate([b_rows] * 4, axis=1).reshape(16 * nd, 128)
     row_b = lax.rem(lax.broadcasted_iota(jnp.int32, (16 * nd, 128), 0), 16) // 4
     b_parts = [jnp.where(row_b == q, b_rows, 0.0).astype(BF16) for q in range(4)]
-    xall_bytes = xall.at[pl.ds(0, len(PLANE))]
-    arrived(xall_bytes, 10)
+    landed(xall.at[pl.ds(0, len(PLANE))], in_sem.at[10])
     z = xall[...].reshape(32 * nd, n_tok // 4)
     for q in range(4):
         added = contract(z, jnp.concatenate([b_parts[q], b_parts[q]], axis=0), 0, 0)
         rows = slice(q * (n_tok // 4), (q + 1) * (n_tok // 4))
         o_out[rows, :] = (keep[chips - 1, rows, :] + adapter_scale * added).astype(BF16)
 
-    sent(stat_r, 0)
-    for n in range(2):
-        chip_copy(n).wait_send()
-        sent(ar.at[n], 2 + 2 * n)
-        full_copy(n).wait_send()
-    sent(gar, 6)
-    sent(gbr, 20)
-    sent(xa_r, 8)
-    sent(xall_bytes, 10)
-    for s in range(chips):
-        pair_copy(s).wait_send()
-    for n in range(len(routes)):
-        part_copy(n).wait_send()
+    tiles = sum(pushed) // 4096
+    deep = max(n for n in range(1, n_tok // 16 + 1) if tiles % n == 0)
+    wide = tiles // deep
+    assert sum(pushed) == tiles * 4096 and wide * 128 <= inner
+    landed(x.at[pl.ds(0, 16 * deep), pl.ds(0, 128 * wide)], out_sem.at[0])
 
     @pl.when(jnp.logical_not(at_home))
     def _():
@@ -442,11 +431,15 @@
 
     @pl.when(at_home)
     def _():
-        for k in range(8):
-
-            @pl.when(8 * core + k != t)
-            def _():
-                column_copy(k).wait_send()
+        among = jnp.logical_and(t >= 8 * core, t < 8 * core + 8)
+
+        @pl.when(among)
+        def _():
+            landed(bc.at[pl.ds(0, 7)], out_sem.at[2])
+
+        @pl.when(jnp.logical_not(among))
+        def _():
+            landed(bc, out_sem.at[2])
 
 
 def hand_over(*refs):
@@ -478,12 +471,11 @@
     quarter, quarter_b = -(-inner // 512) * 128, -(-width // 512) * 128
     rows = rank // nd
     vmem, dma = pltpu.VMEM, pltpu.SemaphoreType.DMA
-    i32 = jnp.int32
     scratch = [
         vmem((tokens, inner), BF16), vmem((tokens, width), BF16),
-        vmem((1, tokens), i32), vmem((1, tokens), i32), vmem((1, tokens), i32),
-        vmem((rank, inner), F32), vmem((rank, inner), F32), vmem((rank, inner), F32),
-        vmem((rank, width), F32), vmem((rank, width), F32), vmem((rank, width), F32),
+        vmem((3, 1, tokens), jnp.int32),
+        vmem((rank, inner), F32), vmem((2, rank, inner), F32),
+        vmem((rank, width), F32), vmem((2, rank, width), F32),
         vmem((chips, inner, 256), BF16), vmem((rollout, inner), BF16),
         vmem((inner, rollout), BF16),
         vmem((4, n_groups), F32), vmem((nd - 1, 4, n_groups), F32),
@@ -500,8 +492,7 @@
         vmem((chips, rollout, 128), F32), vmem((chips, rollout, 128), BF16),
         vmem((chips, rollout, 128), BF16), vmem((7, rollout, 128), BF16),
         vmem((7, rollout, 128), BF16),
-        dma((14,)), dma((chips,)), dma((chips,)), dma((chips,)), dma((7,)), dma((7,)), dma((11,)),
-        dma((22,)),
+        dma((10 + chips,)), dma((3,)), dma((21 + len(ARRIVALS),)),
     ]
     results = [((rollout, 128), BF16)] + [((rows, inner), F32)] * 3 + [((rows, width), F32)] * 3
     held = pl.pallas_call(

time: 33.3 us -> 32.7 us (0.982)
  Pallas kernels: 32.6 us -> 31.9 us
    pallas_call x1, Pallas kernels: 31.8 us -> 31.2 us  [shards(): pl.pallas_call(functools.partial(kernel, nd, nt), out_shape=[vmem(shape,...]
where the time goes in v4:
time: 32.7 us; the launch traced here: 32.6 us
  Pallas kernels  31.9 us (98%)
  between operations  0.65 us (2%)
    pallas_call x1, Pallas kernels, shards(): pl.pallas_call(functools.partial(kernel, nd, nt), out_shape=[vmem(shape,...  31.2 us
    pallas_call x1, Pallas kernels, shards(): pl.pallas_call(hand_over, out_shape=tuple((jax.ShapeDtypeStruct(shape, dt...  0.78 us

profile of v4, /device:TPU:1, one launch (start us, length us, event | category | flops | bytes accessed | tf_op | source)
XLA Modules:
  0.0 32.6 jit_solution(12841782479460330309)
XLA Ops:
  0.6 31.2 %grpo_step.1 = (bf16[512,128]{1,0:T(8,128)(2,1)S(1)}, f32[4,3328]{1,0:T(4,128)S(1)}, f32[4,3328]{1,0:T(4,128)S(1)}, f32[4,3328]{1,0:T(4,128)S(1)}, f32[4,1024]{1...) custom-call(bf16[512,3328]{1,0:T(8,128)(2,1)} %hidden.1, bf16[512,1024]{1,0:T(8,128)(2,1)} %cotangent.1, ...), custom_call_target="tpu_custom_call" | custom-call | tf_op jit(solution)/shard_map/grpo_step/pallas_call | solution.py:498
  31.8 0.8 %hand_over.1 = (bf16[512,128]{1,0:T(8,128)(2,1)}, f32[4,3328]{1,0:T(4,128)}, f32[4,3328]{1,0:T(4,128)}, f32[4,3328]{1,0:T(4,128)}, f32[4,1024]{1,0:T(4,128)}, /*index=5*/f32[4,1024]{1,0:T(4,128)}, f32[4,1024]{1,0:T(4,128)}) custom-call(bf16[512,128]{1,0:T(8,128)(2,1)S(1)} %get-tuple-element.14.refs_0_, f32[4,3328]{1,0:T(4,128)S(1)} %get-tuple-element.15.refs_1_, ...), custom_call_target="tpu_custom_call" | custom-call | tf_op jit(solution)/shard_map/hand_over/pallas_call | solution.py:517

commit v5 on v4

--- a/solution.py
+++ b/solution.py
@@ -365,11 +365,6 @@
     def _():
         home_copy().start()
 
-    for value, ref in zip(adam_a, (o_pa, o_ma, o_va)):
-        split(value, ref, quarter)
-    for value, ref in zip(adam_b, (o_pb, o_mb, o_vb)):
-        split(value, ref, quarter_b)
-
     run(5)
 
     landed(xa_r, in_sem.at[9])
@@ -401,6 +396,11 @@
             @pl.when(here)
             def _():
                 bd[...] = bc[:, :, 128 * k : 128 * k + 128]
+
+    for value, ref in zip(adam_a, (o_pa, o_ma, o_va)):
+        split(value, ref, quarter)
+    for value, ref in zip(adam_b, (o_pb, o_mb, o_vb)):
+        split(value, ref, quarter_b)
 
     keep[chips - 1] = chip_total(chips - 1) + received(4) + received(5) + received(6)
 

time: 32.7 us -> 32.7 us (level)
  no operation moved by 1% of the time
where the time goes in v5:
time: 32.7 us; the launch traced here: 32.6 us
  Pallas kernels  31.9 us (98%)
  between operations  0.65 us (2%)
    pallas_call x1, Pallas kernels, shards(): pl.pallas_call(functools.partial(kernel, nd, nt), out_shape=[vmem(shape,...  31.2 us
    pallas_call x1, Pallas kernels, shards(): pl.pallas_call(hand_over, out_shape=tuple((jax.ShapeDtypeStruct(shape, dt...  0.78 us

profile of v5, /device:TPU:1, one launch (start us, length us, event | category | flops | bytes accessed | tf_op | source)
XLA Modules:
  0.0 32.6 jit_solution(14766794279178183655)
XLA Ops:
  0.6 31.2 %grpo_step.1 = (bf16[512,128]{1,0:T(8,128)(2,1)S(1)}, f32[4,3328]{1,0:T(4,128)S(1)}, f32[4,3328]{1,0:T(4,128)S(1)}, f32[4,3328]{1,0:T(4,128)S(1)}, f32[4,1024]{1...) custom-call(bf16[512,3328]{1,0:T(8,128)(2,1)} %hidden.1, bf16[512,1024]{1,0:T(8,128)(2,1)} %cotangent.1, ...), custom_call_target="tpu_custom_call" | custom-call | tf_op jit(solution)/shard_map/grpo_step/pallas_call | solution.py:498
  31.8 0.8 %hand_over.1 = (bf16[512,128]{1,0:T(8,128)(2,1)}, f32[4,3328]{1,0:T(4,128)}, f32[4,3328]{1,0:T(4,128)}, f32[4,3328]{1,0:T(4,128)}, f32[4,1024]{1,0:T(4,128)}, /*index=5*/f32[4,1024]{1,0:T(4,128)}, f32[4,1024]{1,0:T(4,128)}) custom-call(bf16[512,128]{1,0:T(8,128)(2,1)S(1)} %get-tuple-element.14.refs_0_, f32[4,3328]{1,0:T(4,128)S(1)} %get-tuple-element.15.refs_1_, ...), custom_call_target="tpu_custom_call" | custom-call | tf_op jit(solution)/shard_map/hand_over/pallas_call | solution.py:517
